TPU v7x, 32 devices: a whole 2x2x4 slice. The times are simulated.
32 devices in a mesh: section: 2 (over core), dp: 16 (over z, y, x).
Axes of the slice: x: 2, y: 2, z: 4, core: 2. Of those that a mesh axis runs over, the one named last changes fastest.
Arguments:
- tokens: bfloat16 [16384, 1088], P('dp'), may hold values from -6 to 6
- positions: int32 [16384], P('dp'), may hold values from 0 to 511, as said below
- cotangent: bfloat16 [16384, 1088], P('dp'), may hold values from -6 to 6
- w_qkv: bfloat16 [2, 1088, 3264], P('section', 'dp'), may hold values from -0.1875 to 0.1875
- w_out: bfloat16 [2, 1088, 1088], P('section', 'dp'), may hold values from -1 to 1
- w_up: bfloat16 [2, 1088, 4352], P('section', 'dp'), may hold values from -0.1875 to 0.1875
- w_down: bfloat16 [2, 4352, 1088], P('section', 'dp'), may hold values from -0.09375 to 0.09375
- norm_gains: bfloat16 [2, 2, 1088], P('section', None, 'dp'), may hold values from 0.5 to 1.5
- biases: bfloat16 [2, 6, 1088], P('section', None, 'dp'), may hold values from -3 to 3
- up_bias: bfloat16 [2, 4352], P('section', 'dp'), may hold values from -3 to 3
Outputs:
- section_acts: bfloat16 [2, 16384, 1088], P('section', 'dp')
- section_grads: float32 [2, 16384, 1088], P('section', 'dp')
- grad_qkv: float32 [2, 1088, 3264], P('section', 'dp')
- grad_out: float32 [2, 1088, 1088], P('section', 'dp')
- grad_up: float32 [2, 1088, 4352], P('section', 'dp')
- grad_down: float32 [2, 4352, 1088], P('section', 'dp')
- grad_gains: float32 [2, 2, 1088], P('section', None, 'dp')
- grad_biases: float32 [2, 6, 1088], P('section', None, 'dp')
- grad_up_bias: float32 [2, 4352], P('section', 'dp')
Inputs may be any that keep to these rules, and one draw needn't show every extreme that they name: positions[i] is 0 where a sequence starts and positions[i - 1] + 1 elsewhere; every aligned block of 512 tokens starts a sequence, so no sequence crosses such a block; some block holds a single sequence of 512 tokens.
All inputs are finite; a program needn't handle non-finite values.
Results may differ from a plain program's by a relative error of at most 0.014.
Values may be sent and summed in bfloat16 or wider, within the bound.
No kernel may reach another device: no remote copies, remote signals or barrier semaphores. Data moves between devices by JAX's collectives and lax.ppermute only.
A program may use at most 576 MiB of HBM per device.

v0:
```python
import jax
import jax.numpy as jnp
from jax import lax
from jax.sharding import PartitionSpec as P

D = 1088
HEADS = 17
HEAD_DIM = 64
SEQ = 512
MICRO = 2


EPSILON = 1e-05


def from_behind(x, axis, by):
    devices = lax.axis_size(axis)
    pairs = [(i, i + by) for i in range(devices) if 0 <= i + by < devices]
    return lax.ppermute(x, axis, pairs)


def norm_rows(values, gain_row, shift_row):
    row_mean = jnp.mean(values, axis=-1, keepdims=True)
    centred = values - row_mean
    row_var = jnp.mean(centred * centred, axis=-1, keepdims=True)
    return centred * lax.rsqrt(row_var + EPSILON) * gain_row + shift_row


def permitted(places):
    count = places.shape[0]
    query_idx = jnp.arange(count, dtype=jnp.int32)[:, None]
    key_idx = jnp.arange(count, dtype=jnp.int32)[None, :]
    return (key_idx <= query_idx) & (key_idx >= query_idx - places[:, None])


def outer_sum(left, right):
    return lax.dot_general(
        left, right, (((0,), (0,)), ((), ())), preferred_element_type=jnp.float32
    )


def against(left, right):
    return lax.dot_general(
        left, right, (((1,), (1,)), ((), ())), preferred_element_type=jnp.float32
    )


def masked_scores(heads_qkv, places):
    scores = jnp.einsum(
        "qhd,khd->hqk", heads_qkv[:, 0], heads_qkv[:, 1], preferred_element_type=jnp.float32
    ) * HEAD_DIM ** (-0.5)
    return jnp.where(permitted(places)[None], scores, -jnp.inf)


def run_forward(operand):
    source, places, weights = operand
    w_qkv, w_out, w_up, w_down, gains, shifts, up_bias = weights
    gain_vals = gains.astype(jnp.float32)
    shift_vals = shifts.astype(jnp.float32)
    input_rows = source.astype(jnp.float32)
    count, feat_width = input_rows.shape
    normed_one = norm_rows(input_rows, gain_vals[0], shift_vals[0]).astype(jnp.bfloat16)
    qkv_bias = jnp.concatenate([shift_vals[1], jnp.zeros_like(shift_vals[1]), shift_vals[2]])
    joined = (jnp.dot(normed_one, w_qkv, preferred_element_type=jnp.float32) + qkv_bias).astype(
        jnp.bfloat16
    )
    heads_qkv = joined.reshape(count, 3, HEADS, HEAD_DIM)
    masked = masked_scores(heads_qkv, places)
    row_top = jnp.max(masked, axis=-1, keepdims=True)
    expo_vals = jnp.exp(masked - row_top)
    row_total = jnp.sum(expo_vals, axis=-1, keepdims=True)
    soft_low = (expo_vals / row_total).astype(jnp.bfloat16)
    mixed_heads = jnp.einsum(
        "hqk,khd->qhd", soft_low, heads_qkv[:, 2], preferred_element_type=jnp.float32
    )
    mixed_heads = mixed_heads.reshape(count, feat_width).astype(jnp.bfloat16)
    hidden_one = input_rows + (
        jnp.dot(mixed_heads, w_out, preferred_element_type=jnp.float32) + shift_vals[3]
    )
    normed_two = norm_rows(hidden_one, gain_vals[1], shift_vals[4]).astype(jnp.bfloat16)
    inner_pre = jnp.dot(normed_two, w_up, preferred_element_type=jnp.float32) + up_bias.astype(
        jnp.float32
    )
    active = jax.nn.gelu(inner_pre, approximate=False).astype(jnp.bfloat16)
    result = hidden_one + (
        jnp.dot(active, w_down, preferred_element_type=jnp.float32) + shift_vals[5]
    )
    kept_state = (
        input_rows,
        normed_one,
        joined,
        row_top,
        row_total,
        mixed_heads,
        hidden_one,
        normed_two,
        inner_pre,
        active,
    )
    return (result, kept_state)


def blank_forward(operand):
    source, places, weights = operand
    count, feat_width = source.shape
    hidden_width = weights[2].shape[1]
    dense = jnp.zeros((count, feat_width), jnp.float32)
    narrow = jnp.zeros((count, feat_width), jnp.bfloat16)
    stats = jnp.zeros((HEADS, count, 1), jnp.float32)
    totals_one = jnp.ones((HEADS, count, 1), jnp.float32)
    kept_state = (
        dense,
        narrow,
        jnp.zeros((count, 3 * feat_width), jnp.bfloat16),
        stats,
        totals_one,
        narrow,
        dense,
        narrow,
        jnp.zeros((count, hidden_width), jnp.float32),
        jnp.zeros((count, hidden_width), jnp.bfloat16),
    )
    return (dense, kept_state)


def back_mlp(grad_rows, weights, kept_state):
    w_qkv, w_out, w_up, w_down, gains, shifts, up_bias = weights
    gain_vals = gains.astype(jnp.float32)
    shift_vals = shifts.astype(jnp.float32)
    (
        input_rows,
        normed_one,
        joined,
        row_top,
        row_total,
        mixed_heads,
        hidden_one,
        normed_two,
        inner_pre,
        active,
    ) = kept_state
    down_in = grad_rows.astype(jnp.bfloat16)
    grad_wdown = outer_sum(active, down_in)
    grad_bdown = jnp.sum(down_in, axis=0, dtype=jnp.float32)
    d_active = against(down_in, w_down)
    unused_gelu, gelu_back = jax.vjp(
        lambda values_in: jax.nn.gelu(values_in, approximate=False), inner_pre
    )
    d_inner = gelu_back(d_active)[0].astype(jnp.bfloat16)
    grad_wup = outer_sum(normed_two, d_inner)
    grad_bup = jnp.sum(d_inner, axis=0, dtype=jnp.float32)
    d_second = against(d_inner, w_up)
    unused_two, second_back = jax.vjp(norm_rows, hidden_one, gain_vals[1], shift_vals[4])
    d_hidden, grad_gain_two, grad_shift_two = second_back(d_second)
    d_hidden = grad_rows + d_hidden
    return (d_hidden, (grad_wdown, grad_bdown, grad_wup, grad_bup, grad_gain_two, grad_shift_two))


def back_attention(d_hidden, places, weights, kept_state):
    w_qkv, w_out, w_up, w_down, gains, shifts, up_bias = weights
    gain_vals = gains.astype(jnp.float32)
    shift_vals = shifts.astype(jnp.float32)
    (
        input_rows,
        normed_one,
        joined,
        row_top,
        row_total,
        mixed_heads,
        hidden_one,
        normed_two,
        inner_pre,
        active,
    ) = kept_state
    count, feat_width = input_rows.shape
    out_in = d_hidden.astype(jnp.bfloat16)
    grad_wout = outer_sum(mixed_heads, out_in)
    grad_bout = jnp.sum(out_in, axis=0, dtype=jnp.float32)
    d_mixed = against(out_in, w_out).astype(jnp.bfloat16).reshape(count, HEADS, HEAD_DIM)
    heads_qkv = joined.reshape(count, 3, HEADS, HEAD_DIM)
    masked = masked_scores(heads_qkv, places)
    weights_soft = jnp.exp(masked - row_top) / row_total
    soft_low = weights_soft.astype(jnp.bfloat16)
    d_values = jnp.einsum("hqk,qhd->khd", soft_low, d_mixed, preferred_element_type=jnp.float32)
    d_soft = jnp.einsum(
        "qhd,khd->hqk", d_mixed, heads_qkv[:, 2], preferred_element_type=jnp.float32
    )
    d_scores = (
        weights_soft * (d_soft - jnp.sum(d_soft * weights_soft, axis=-1, keepdims=True))
    ).astype(jnp.bfloat16)
    score_scale = HEAD_DIM ** (-0.5)
    d_query = (
        jnp.einsum("hqk,khd->qhd", d_scores, heads_qkv[:, 1], preferred_element_type=jnp.float32)
        * score_scale
    )
    d_keys = (
        jnp.einsum("hqk,qhd->khd", d_scores, heads_qkv[:, 0], preferred_element_type=jnp.float32)
        * score_scale
    )
    d_joined = (
        jnp.stack([d_query, d_keys, d_values], axis=1)
        .reshape(count, 3 * feat_width)
        .astype(jnp.bfloat16)
    )
    grad_wqkv = outer_sum(normed_one, d_joined)
    joined_sums = jnp.sum(d_joined, axis=0, dtype=jnp.float32)
    d_first = against(d_joined, w_qkv)
    unused_one, first_back = jax.vjp(norm_rows, input_rows, gain_vals[0], shift_vals[0])
    d_input, grad_gain_one, grad_shift_one = first_back(d_first)
    d_input = d_hidden + d_input
    return (d_input, (grad_wqkv, grad_wout, grad_gain_one, grad_shift_one, joined_sums, grad_bout))


def assemble(mlp_part, attention_part):
    grad_wdown, grad_bdown, grad_wup, grad_bup, grad_gain_two, grad_shift_two = mlp_part
    grad_wqkv, grad_wout, grad_gain_one, grad_shift_one, joined_sums, grad_bout = attention_part
    feat_width = grad_bout.shape[0]
    grad_gain_rows = jnp.stack([grad_gain_one, grad_gain_two])
    grad_shift_rows = jnp.stack(
        [
            grad_shift_one,
            joined_sums[:feat_width],
            joined_sums[2 * feat_width :],
            grad_bout,
            grad_shift_two,
            grad_bdown,
        ]
    )
    return (grad_wqkv, grad_wout, grad_wup, grad_wdown, grad_gain_rows, grad_shift_rows, grad_bup)


def run_backward(operand):
    grad_rows, places, weights, kept_state = operand
    d_hidden, mlp_part = back_mlp(grad_rows, weights, kept_state)
    d_input, attention_part = back_attention(d_hidden, places, weights, kept_state)
    return (d_input, assemble(mlp_part, attention_part))


def blank_backward(operand):
    grad_rows, places, weights, kept_state = operand
    return (
        jnp.zeros(grad_rows.shape, jnp.float32),
        jax.tree.map(lambda item: jnp.zeros(item.shape, jnp.float32), weights),
    )


def per_device(
    tokens, positions, cotangent, w_qkv, w_out, w_up, w_down, norm_gains, biases, up_bias
):
    section_index = lax.axis_index("section")
    first_section = section_index == 0
    row_count = SEQ
    gathered = (
        lax.all_gather(w_qkv, "dp", axis=1, tiled=True),
        lax.all_gather(w_out, "dp", axis=1, tiled=True),
        lax.all_gather(w_up, "dp", axis=1, tiled=True),
        lax.all_gather(w_down, "dp", axis=1, tiled=True),
        lax.all_gather(norm_gains, "dp", axis=2, tiled=True),
        lax.all_gather(biases, "dp", axis=2, tiled=True),
        lax.all_gather(up_bias, "dp", axis=1, tiled=True),
    )
    layer_weights = tuple((item[0] for item in gathered))
    incoming = jnp.zeros((row_count, D), jnp.bfloat16)
    results = []
    stores = []
    for step_index in range(MICRO + 1):
        if step_index < MICRO:
            fresh_rows = tokens[step_index * row_count : (step_index + 1) * row_count]
        else:
            fresh_rows = jnp.zeros((row_count, D), jnp.bfloat16)
        source = jnp.where(first_section, fresh_rows, incoming)
        batch_index = step_index - section_index
        is_valid = (batch_index >= 0) & (batch_index < MICRO)
        place_start = jnp.clip(batch_index, 0, MICRO - 1) * row_count
        places = lax.dynamic_slice_in_dim(positions, place_start, row_count)
        result, kept_state = lax.cond(
            is_valid, run_forward, blank_forward, (source, places, layer_weights)
        )
        outgoing = result.astype(jnp.bfloat16)
        results.append(outgoing)
        stores.append(kept_state)
        if step_index < MICRO:
            incoming = from_behind(outgoing, "section", 1)
    regathered = (
        lax.all_gather(w_qkv, "dp", axis=1, tiled=True),
        lax.all_gather(w_out, "dp", axis=1, tiled=True),
        lax.all_gather(w_up, "dp", axis=1, tiled=True),
        lax.all_gather(w_down, "dp", axis=1, tiled=True),
        lax.all_gather(norm_gains, "dp", axis=2, tiled=True),
        lax.all_gather(biases, "dp", axis=2, tiled=True),
        lax.all_gather(up_bias, "dp", axis=1, tiled=True),
    )
    layer_weights = tuple((item[0] for item in regathered))
    returning = jnp.zeros((row_count, D), jnp.bfloat16)
    grad_inputs = []
    totals = jax.tree.map(lambda item: jnp.zeros(item.shape, jnp.float32), layer_weights)
    owned = None
    for step_index in range(MICRO + 1):
        later_index = MICRO - 1 - step_index
        if step_index < MICRO:
            given_rows = cotangent[later_index * row_count : (later_index + 1) * row_count]
        else:
            given_rows = jnp.zeros((row_count, D), jnp.bfloat16)
        grad_rows = jnp.where(first_section, returning, given_rows).astype(jnp.float32)
        batch_index = MICRO - step_index - section_index
        is_valid = (batch_index >= 0) & (batch_index < MICRO)
        place_start = jnp.clip(batch_index, 0, MICRO - 1) * row_count
        places = lax.dynamic_slice_in_dim(positions, place_start, row_count)
        kept_state = stores[MICRO - step_index]
        d_input, layer_grads = lax.cond(
            is_valid, run_backward, blank_backward, (grad_rows, places, layer_weights, kept_state)
        )
        grad_inputs.append(d_input)
        totals = jax.tree.map(jnp.add, totals, layer_grads)
        if step_index < MICRO:
            returning = from_behind(d_input.astype(jnp.bfloat16), "section", -1)
    owned = (
        lax.psum_scatter(totals[0][None], "dp", scatter_dimension=1, tiled=True),
        lax.psum_scatter(totals[1][None], "dp", scatter_dimension=1, tiled=True),
        lax.psum_scatter(totals[2][None], "dp", scatter_dimension=1, tiled=True),
        lax.psum_scatter(totals[3][None], "dp", scatter_dimension=1, tiled=True),
        lax.psum_scatter(totals[4][None], "dp", scatter_dimension=2, tiled=True),
        lax.psum_scatter(totals[5][None], "dp", scatter_dimension=2, tiled=True),
        lax.psum_scatter(totals[6][None], "dp", scatter_dimension=1, tiled=True),
    )
    acts_rows = jnp.concatenate(
        [jnp.where(first_section, results[index], results[index + 1]) for index in range(MICRO)],
        axis=0,
    )
    grad_rows_out = jnp.concatenate(
        [
            jnp.where(first_section, grad_inputs[MICRO - index], grad_inputs[MICRO - 1 - index])
            for index in range(MICRO)
        ],
        axis=0,
    )
    return (
        acts_rows[None],
        grad_rows_out[None],
        owned[0],
        owned[1],
        owned[2],
        owned[3],
        owned[4],
        owned[5],
        owned[6],
    )


def solution(mesh):
    in_specs = (
        P("dp", None),
        P("dp"),
        P("dp", None),
        P("section", "dp", None),
        P("section", "dp", None),
        P("section", "dp", None),
        P("section", "dp", None),
        P("section", None, "dp"),
        P("section", None, "dp"),
        P("section", "dp"),
    )
    out_specs = (
        P("section", "dp", None),
        P("section", "dp", None),
        P("section", "dp", None),
        P("section", "dp", None),
        P("section", "dp", None),
        P("section", "dp", None),
        P("section", None, "dp"),
        P("section", None, "dp"),
        P("section", "dp"),
    )
    return jax.shard_map(
        per_device, mesh=mesh, in_specs=in_specs, out_specs=out_specs, check_vma=False
    )
```

profile of v0, /device:TPU:0, one launch (start us, length us, event | category | flops | bytes accessed | tf_op | source)
XLA Modules:
  0.0 3180.5 jit_solution(17755774926424492623)
XLA Ops:
  15.8 49.2 %all_gather.26 = bf16[1,2,1088]{1,0,2:T(2,128)(2,1)S(1)} all-gather(bf16[1,2,68]{1,0,2:T(2,128)(2,1)S(1)} %copy.192), channel_id=1, replica_groups=mesh['section'=2,'dp'=16] {'dp'}, dimensions={2}, use_global_device_ids=true | all-gather | bytes 4624 | tf_op jit(solution)/shard_map/all_gather | solution.py:258
  65.9 42.4 %all_gather.27 = bf16[1,6,1088]{1,0,2:T(2,128)(2,1)S(1)} all-gather(bf16[1,6,68]{1,0,2:T(2,128)(2,1)S(1)} %copy.194), channel_id=1, replica_groups=mesh['section'=2,'dp'=16] {'dp'}, dimensions={2}, use_global_device_ids=true | all-gather | bytes 13872 | tf_op jit(solution)/shard_map/all_gather | solution.py:259
  110.7 75.6 %all-reduce = bf16[4352]{0:T(1024)(128)(2,1)S(1)} all-reduce(bf16[4352]{0:T(1024)(128)(2,1)S(1)} %dynamic-update-slice), channel_id=1, replica_groups=mesh['section'=2,'dp'=16] {'dp'}, use_global_device_ids=true, to_apply=%add | all-reduce | flops 4352 | bytes 17408 | tf_op jit(solution)/shard_map/squeeze | solution.py:262
  191.2 90.3 %all-gather.5.cloned.1.call-done = bf16[1,1088,3264]{2,0,1:T(2,128)(2,1)} async-done(((bf16[1,68,3264]{2,0,1:T(2,128)(2,1)}), bf16[1,1088,3264]{2,0,1:T(2,128)(2,1)}) %all-gather.5.cloned.1.call-update) | async-done | bytes 7102480 | tf_op jit(solution)/shard_map/all_gather | solution.py:254
  290.6 204.4 %all-gather.9.cloned.1.call-done = bf16[1,1088,4352]{2,0,1:T(2,128)(2,1)} async-done(((bf16[1,68,4352]{2,0,1:T(2,128)(2,1)}), bf16[1,1088,4352]{2,0,1:T(2,128)(2,1)}) %all-gather.9.cloned.1.call-update) | async-done | bytes 9469968 | tf_op jit(solution)/shard_map/all_gather | solution.py:256
  509.0 114.8 %all-gather.11.cloned.1.call-done = bf16[1,4352,1088]{2,1,0:T(8,128)(2,1)} async-done(((bf16[1,272,1088]{2,1,0:T(8,128)(2,1)}), bf16[1,4352,1088]{2,1,0:T(8,128)(2,1)}) %all-gather.11.cloned.1.call-update) | async-done | bytes 9469968 | tf_op jit(solution)/shard_map/all_gather | solution.py:257
  623.8 97.2 %conditional.6 = (f32[512,1088]{0,1:T(8,128)S(1)}, bf16[512,1088]{0,1:T(8,128)(2,1)}, bf16[512,3264]{0,1:T(8,128)(2,1)}, f32[17,512,1]{1,0,2:T(8,128)}, f32[17,5...) conditional(s32[]{:T(128)} %convert_element_type.279, () %tuple.62, ...), branch_computations={%region_0.1_spmd, %region_1.8_spmd} | conditional | flops 15905846272 | bytes 164374272 | solution.py:276
  677.1 29.6 fusion.4
  725.0 99.7 %conditional.7 = (f32[512,1088]{0,1:T(8,128)}, bf16[512,1088]{0,1:T(8,128)(2,1)}, bf16[512,3264]{0,1:T(8,128)(2,1)}, f32[17,512,1]{1,0,2:T(8,128)}, f32[17,512,1...) conditional(s32[]{:T(128)} %convert_element_type.280, () %tuple.64, ...), branch_computations={%region_8.9_spmd, %region_9.16_spmd} | conditional | flops 15905846272 | bytes 173909760 | solution.py:276
  783.5 28.0 fusion.25
  850.0 36.7 %conditional.9 = (f32[512,1088]{0,1:T(8,128)}, f32[1088,3264]{1,0:T(8,128)}, f32[1088,4352]{1,0:T(8,128)}, f32[4352,1088]{0,1:T(8,128)}, f32[2,1088]{1,0:T(2,128...) conditional(s32[]{:T(128)} %convert_element_type.281, () %tuple.70, (f32[512,4352]{1,0:T(8,128)}, ...), branch_computations={%region_24.25_spmd, %region_25.43_spmd} | conditional | flops 32195272704 | bytes 436097632 | solution.py:310
  889.8 208.8 %collective-permute-done.2 = bf16[512,1088]{0,1:T(8,128)(2,1)S(1)} collective-permute-done((bf16[512,1088]{0,1:T(8,128)(2,1)S(1)}, bf16[512,1088]{0,1:T(8,128)(2,1)S(1)}, u32[]{:S(2)}, u32[]{:S(2)}) %collective-permute-start.2) | collective-permute-done | bytes 1114144 | tf_op jit(solution)/shard_map/ppermute | solution.py:19
  1100.1 164.5 %conditional.10 = (f32[512,1088]{0,1:T(8,128)}, f32[1088,3264]{1,0:T(8,128)}, f32[1088,4352]{1,0:T(8,128)}, f32[4352,1088]{0,1:T(8,128)}, f32[2,1088]{1,0:T(2,12...) conditional(s32[]{:T(128)} %convert_element_type.280, () %tuple.69, ...), branch_computations={%region_43.44_spmd, %region_44.62_spmd} | conditional | flops 32195272704 | bytes 431641184 | solution.py:310
  1104.6 29.6 convert_reduce_fusion.4
  1274.7 162.0 %conditional.11 = (f32[512,1088]{0,1:T(8,128)}, f32[1088,3264]{1,0:T(8,128)}, f32[1088,4352]{1,0:T(8,128)}, f32[4352,1088]{0,1:T(8,128)}, f32[2,1088]{1,0:T(2,12...) conditional(s32[]{:T(128)} %convert_element_type.279, () %tuple.68, (f32[512,4352]{1,0:T(8,128)}, ...), branch_computations={%region_62.63_spmd, %region_63.81_spmd} | conditional | flops 32195272704 | bytes 436097632 | solution.py:310
  1279.4 30.9 convert_reduce_fusion.8
  1491.9 25.5 add_bitcast_fusion
  1517.4 42.3 %copy.211 = f32[1,4352,1088]{2,0,1:T(1,128)} copy(f32[1,4352,1088]{1,2,0:T(8,128)} %add_bitcast_fusion) | data formatting | bytes 37879808 | tf_op jit(solution)/shard_map/broadcast_in_dim | solution.py:321
  1559.8 26.1 add_add_fusion.12
  1585.9 21.4 broadcast_in_dim.194
  1610.4 74.8 %all-reduce.7 = (f32[1,2,1088]{2,1,0:T(2,128)S(1)}, f32[1,6,1088]{2,0,1:T(1,128)S(1)}) all-reduce(f32[1,2,1088]{2,1,0:T(2,128)S(1)} %add_bitcast_fusion.1, f32[1,6,1088]{2,0,1:T(1,128)S(1)} %broadcast_in_dim.197), channel_id=6, replica_groups=mesh['section'=2,'dp'=16] {'dp'}, use_global_device_ids=true, to_apply=%region_85.86.clone | all-reduce | flops 8704 | bytes 69632
  1711.1 408.0 %all-reduce.13.cloned.1.call-done = f32[1,1088,3264]{2,0,1:T(1,128)} async-done(((f32[1,1088,3264]{2,0,1:T(1,128)}), f32[1,1088,3264]{2,0,1:T(1,128)}) %all-reduce.13.cloned.1.call-update) | async-done | bytes 14204944
  2121.2 535.6 %all-reduce.19.cloned.1.call-done = f32[1,4352,1088]{2,0,1:T(1,128)} async-done(((f32[1,4352,1088]{2,0,1:T(1,128)}), f32[1,4352,1088]{2,0,1:T(1,128)}) %all-reduce.19.cloned.1.call-update) | async-done | bytes 18939920
  2660.1 511.3 %all-reduce.17.cloned.1.call-done = f32[1,1088,4352]{2,0,1:T(1,128)} async-done(((f32[1,1088,4352]{2,0,1:T(1,128)}), f32[1,1088,4352]{2,0,1:T(1,128)}) %all-reduce.17.cloned.1.call-update) | async-done | bytes 18939920
  (328 shorter events, 619.3 us)
Async XLA Ops:
  7.2 101.9 %copy-start.53 = (u32[32]{0:T(128)S(1)}, u32[32]{0:T(128)}, u32[]{:S(2)}) copy-start(u32[32]{0:T(128)} %constant.555) | copy-start | bytes 388
  7.2 101.9 %copy-start.54 = (bf16[1,272]{1,0:T(2,128)(2,1)S(1)}, bf16[1,272]{1,0:T(2,128)(2,1)}, u32[]{:S(2)}) copy-start(bf16[1,272]{1,0:T(2,128)(2,1)} %param.31) | copy-start | bytes 1636
  7.2 179.0 %copy-start.51 = (s32[1024]{0:T(1024)S(1)}, s32[1024]{0:T(1024)}, u32[]{:S(2)}) copy-start(s32[1024]{0:T(1024)} %param.23) | copy-start | bytes 12292
  7.2 179.7 %all-gather.7.cloned.1.call-start = ((), (), s32[]{:S(2)}) async-start(), calls=%async_computation.2 | async-start | bytes 5326848 | tf_op jit(solution)/shard_map/all_gather | solution.py:255
  9.2 272.3 %all-gather.5.cloned.1.call-start = ((), (), s32[]{:S(2)}) async-start(), calls=%async_computation.1 | async-start | bytes 15388672 | tf_op jit(solution)/shard_map/all_gather | solution.py:254
  11.9 483.1 %all-gather.9.cloned.1.call-start = ((), (), s32[]{:S(2)}) async-start(), calls=%async_computation.3 | async-start | bytes 20123648 | tf_op jit(solution)/shard_map/all_gather | solution.py:256
  15.0 608.8 %all-gather.11.cloned.1.call-start = ((), (), s32[]{:S(2)}) async-start(), calls=%async_computation.4 | async-start | bytes 10653696 | tf_op jit(solution)/shard_map/all_gather | solution.py:257
  15.6 1678.2 %reduce-scatter.6.cloned.1.call-start = ((), (), s32[]{:S(2)}) async-start(), calls=%async_computation.5 | async-start | bytes 2367488
  186.9 436.9 %copy-start.46 = (s32[512]{0:T(512)}, s32[512]{0:T(512)S(1)}, u32[]{:S(2)}) copy-start(s32[512]{0:T(512)S(1)} %get-tuple-element.897) | copy-start | bytes 6148
  186.9 538.1 %copy-start.48 = (s32[512]{0:T(512)}, s32[512]{0:T(512)S(1)}, u32[]{:S(2)}) copy-start(s32[512]{0:T(512)S(1)} %get-tuple-element.898) | copy-start | bytes 6148
  721.0 4.0 collective-permute-start
  725.0 106.2 %copy-start.50 = (s32[512]{0:T(512)S(1)}, s32[512]{0:T(512)}, u32[]{:S(2)}) copy-start(s32[512]{0:T(512)} %get-tuple-element.896) | copy-start | bytes 6148
  824.8 6.4 collective-permute-start.1
  886.7 213.3 %copy-start.32 = (f32[17,512,1]{1,0,2:T(8,128)S(1)}, f32[17,512,1]{1,0,2:T(8,128)}, u32[]{:S(2)}) copy-start(f32[17,512,1]{1,0,2:T(8,128)} %get-tuple-element.347) | copy-start | bytes 104452
  886.7 213.3 %copy-start.43 = (f32[17,512,1]{1,0,2:T(8,128)S(1)}, f32[17,512,1]{1,0,2:T(8,128)}, u32[]{:S(2)}) copy-start(f32[17,512,1]{1,0,2:T(8,128)} %get-tuple-element.348) | copy-start | bytes 104452
  886.7 213.3 %copy-start.49 = (s32[512]{0:T(512)S(1)}, s32[512]{0:T(512)}, u32[]{:S(2)}) copy-start(s32[512]{0:T(512)} %copy-done.48) | copy-start | bytes 6148
  888.5 210.1 %collective-permute-start.2 = (bf16[512,1088]{0,1:T(8,128)(2,1)S(1)}, bf16[512,1088]{0,1:T(8,128)(2,1)S(1)}, u32[]{:S(2)}, u32[]{:S(2)}) collective-permute-start(bf16[512,1088]{0,1:T(8,128)(2,1)S(1)} %convert_element_type.283), channel_id=1, source_target_pairs={{16,0},{17,1},{18,2},{19,3},{20,4},{21,5},{22,6},{23,7},{24,8},{25... | collective-permute-start | bytes 3342344 | tf_op jit(solution)/shard_map/ppermute | solution.py:19
  1100.1 171.1 %copy-start.17 = (bf16[512,1088]{0,1:T(8,128)(2,1)S(1)}, bf16[512,1088]{0,1:T(8,128)(2,1)}, u32[]{:S(2)}) copy-start(bf16[512,1088]{0,1:T(8,128)(2,1)} %copy-done.16) | copy-start | bytes 3342340
  1266.4 4.8 collective-permute-start.3
  1274.7 162.0 %copy-start.36 = (f32[4352]{0:T(1024)S(1)}, f32[4352]{0:T(1024)}, u32[]{:S(2)}) copy-start(f32[4352]{0:T(1024)} %copy-done.35) | copy-start | bytes 52228
  1439.6 269.8 %all-reduce.15.cloned.1.call-start = ((), (), s32[]{:S(2)}) async-start(), calls=%async_computation.7 | async-start | bytes 10027008
  1453.3 665.7 %all-reduce.13.cloned.1.call-start = ((), (), s32[]{:S(2)}) async-start(), calls=%async_computation.6 | async-start | bytes 28966912
  1491.8 1165.0 %all-reduce.19.cloned.1.call-start = ((), (), s32[]{:S(2)}) async-start(), calls=%async_computation.9 | async-start | bytes 40108032
  1559.8 1611.6 %all-reduce.17.cloned.1.call-start = ((), (), s32[]{:S(2)}) async-start(), calls=%async_computation.8 | async-start | bytes 37879808
  (41 other events, 617.8 us)
Sparse Core Ops, SparseCore 0:
  11.3 96.0 all-gather.6
  110.8 170.5 all-gather.4
  284.7 210.2 all-gather.8
  497.7 126.0 all-gather.10
  1439.7 78.9 reduce-scatter.5
  1525.4 183.8 all-reduce.14
  1716.9 402.1 all-reduce.12
  2125.5 531.3 all-reduce.18
  2664.4 506.9 all-reduce.16
where the time goes:
time: 3190 us; the launch traced here: 3180 us
  waiting for transfers between devices  2090 us (66%)
  matrix products  402 us (13%)
  blocking collectives  242 us (8%)
  local copies, waits for them, and re-layouts  203 us (6%)
  other arithmetic  201 us (6%)
    unnamed x14, waiting for transfers between devices  1470 us
    ppermute x4, waiting for transfers between devices, from_behind(): return lax.ppermute(x, axis, pairs)  214 us
    all_gather x1, waiting for transfers between devices, per_device(): lax.all_gather(w_up, 'dp', axis=1, tiled=True)  204 us
    all_gather x1, waiting for transfers between devices, per_device(): lax.all_gather(w_down, 'dp', axis=1, tiled=True)  115 us
    dot_general x8, matrix products, against(): lax.dot_general(left, right, (((1,), (1,)), ((), ())), preferred_element_...  97.1 us
    all_gather x1, waiting for transfers between devices, per_device(): lax.all_gather(w_qkv, 'dp', axis=1, tiled=True)  90.3 us
    squeeze x1, blocking collectives, per_device(): layer_weights = tuple((item[0] for item in gathered))  75.6 us
    unnamed x1, blocking collectives  74.8 us
  transfers between devices with their start and end apart: 13, of which 10 were waited for; matrix products, arithmetic and copies ran while one was open for 7% of the time, Pallas kernels for 0%

commit v1 on v0

v1 whole, which is shorter than its diff:
```python
import jax
import jax.numpy as jnp
from jax import lax
from jax.sharding import PartitionSpec as P

HEAD_DIM = 64
EPSILON = 1e-05
BOTH = ("section", "dp")
F32 = jnp.float32
BF16 = jnp.bfloat16


def norm_rows(values, gain_row, shift_row):
    row_mean = jnp.mean(values, axis=-1, keepdims=True)
    centred = values - row_mean
    row_var = jnp.mean(centred * centred, axis=-1, keepdims=True)
    return centred * lax.rsqrt(row_var + EPSILON) * gain_row + shift_row


def permitted(places):
    count = places.shape[0]
    query_idx = jnp.arange(count, dtype=jnp.int32)[:, None]
    key_idx = jnp.arange(count, dtype=jnp.int32)[None, :]
    return (key_idx <= query_idx) & (key_idx >= query_idx - places[:, None])


def product(left, right):
    return jnp.dot(left, right, preferred_element_type=F32)


def outer_sum(left, right):
    return lax.dot_general(left, right, (((0,), (0,)), ((), ())), preferred_element_type=F32)


def against(left, right):
    return lax.dot_general(left, right, (((1,), (1,)), ((), ())), preferred_element_type=F32)


class Links:
    def __init__(self, data_devices):
        self.count = data_devices
        self.core = lax.axis_index("section")
        self.me = lax.axis_index("dp")
        self.deep = data_devices // 4
        self.staged = data_devices == 16
        quad = self.me % 4
        self.level = self.me // 4
        flip_first = jnp.where(self.core == 0, 2, 1)
        self.quad = quad
        self.quad_first = quad ^ flip_first
        self.quad_second = quad ^ (3 - flip_first)
        self.quad_far = quad ^ 3
        count = data_devices
        index = [(c, d) for c in range(2) for d in range(count)]

        def pairs(move):
            return [(c * count + d, move(c, d)) for c, d in index]

        self.swap = pairs(lambda c, d: (1 - c) * count + d)
        self.first = pairs(lambda c, d: c * count + (d ^ (2 if c == 0 else 1)))
        self.second = pairs(lambda c, d: c * count + (d ^ (1 if c == 0 else 2)))
        self.turns = [
            pairs(lambda c, d, k=k: c * count + (d + 4 * k) % count) for k in range(self.deep)
        ]

    def send(self, x, perm):
        return lax.ppermute(x, BOTH, perm)

    def swap_cores(self, x):
        return self.send(x, self.swap)

    def gather(self, half):
        if not self.staged:
            return lax.all_gather(half, "dp", axis=0)
        deep = self.deep
        turned = [half] + [self.send(half, self.turns[k]) for k in range(1, deep)]
        listed = jnp.stack([turned[(-t) % deep] for t in range(2 * deep)])
        mine = lax.dynamic_slice_in_dim(listed, deep - self.level, deep, 0)
        second = self.send(mine, self.second)
        pair = jnp.stack([mine, second])
        far = self.send(pair, self.first)
        out = jnp.zeros((deep, 4) + half.shape, half.dtype)
        for part, place in (
            (mine, self.quad),
            (second, self.quad_second),
            (far[0], self.quad_first),
            (far[1], self.quad_far),
        ):
            out = lax.dynamic_update_slice_in_dim(out, part[:, None], place, 1)
        return out.reshape((self.count,) + half.shape)

    def reduce(self, total):
        if not self.staged:
            return lax.psum_scatter(total.astype(F32), "dp", scatter_dimension=0)
        deep = self.deep
        shape = total.shape[1:]
        quads = total.reshape((deep, 4) + shape)

        def pick(place):
            return lax.dynamic_slice_in_dim(quads, place, 1, 1)[:, 0]

        arrived = self.send(jnp.stack([pick(self.quad_first), pick(self.quad_far)]), self.first)
        passed = (pick(self.quad_second).astype(F32) + arrived[1].astype(F32)).astype(BF16)
        kept = pick(self.quad).astype(F32) + arrived[0].astype(F32)
        arrived = self.send(passed, self.second)
        kept = (kept + arrived.astype(F32)).astype(BF16)

        def block(step):
            place = (self.level + step) % deep
            return lax.dynamic_slice_in_dim(kept, place, 1, 0)[0]

        result = block(0).astype(F32)
        for k in range(1, deep):
            result = result + self.send(block(k), self.turns[k]).astype(F32)
        return result


def masked_scores(heads_qkv, places):
    scores = jnp.einsum(
        "qhd,khd->hqk", heads_qkv[:, 0], heads_qkv[:, 1], preferred_element_type=F32
    ) * HEAD_DIM ** (-0.5)
    return jnp.where(permitted(places)[None], scores, -jnp.inf)


def attend(joined, places):
    count, wide = joined.shape
    heads_qkv = joined.reshape(count, 3, -1, HEAD_DIM)
    masked = masked_scores(heads_qkv, places)
    row_top = jnp.max(masked, axis=-1, keepdims=True)
    expo_vals = jnp.exp(masked - row_top)
    row_total = jnp.sum(expo_vals, axis=-1, keepdims=True)
    soft_low = (expo_vals / row_total).astype(BF16)
    mixed = jnp.einsum("hqk,khd->qhd", soft_low, heads_qkv[:, 2], preferred_element_type=F32)
    return mixed.reshape(count, wide // 3).astype(BF16), (row_top, row_total)


def attend_back(joined, places, stats, d_mixed):
    count, wide = joined.shape
    row_top, row_total = stats
    heads_qkv = joined.reshape(count, 3, -1, HEAD_DIM)
    d_mixed = d_mixed.reshape(count, -1, HEAD_DIM)
    masked = masked_scores(heads_qkv, places)
    weights_soft = jnp.exp(masked - row_top) / row_total
    soft_low = weights_soft.astype(BF16)
    d_values = jnp.einsum("hqk,qhd->khd", soft_low, d_mixed, preferred_element_type=F32)
    d_soft = jnp.einsum("qhd,khd->hqk", d_mixed, heads_qkv[:, 2], preferred_element_type=F32)
    d_scores = (
        weights_soft * (d_soft - jnp.sum(d_soft * weights_soft, axis=-1, keepdims=True))
    ).astype(BF16)
    scale = HEAD_DIM ** (-0.5)
    d_query = (
        jnp.einsum("hqk,khd->qhd", d_scores, heads_qkv[:, 1], preferred_element_type=F32) * scale
    )
    d_keys = (
        jnp.einsum("hqk,qhd->khd", d_scores, heads_qkv[:, 0], preferred_element_type=F32) * scale
    )
    return jnp.stack([d_query, d_keys, d_values], axis=1).reshape(count, wide).astype(BF16)


def layer_forward(source, places, weights, spread):
    w_qo, w_up, w_down, gains, shifts, up_bias = weights
    feat = source.shape[1]
    rows = source.astype(F32)
    normed_one = norm_rows(rows, gains[0], shifts[0]).astype(BF16)
    normed_one = product(normed_one, spread).astype(BF16)
    bias = jnp.concatenate([shifts[1], jnp.zeros_like(shifts[1]), shifts[2]])
    joined = (product(normed_one, w_qo)[:, : 3 * feat] + bias).astype(BF16)
    mixed, stats = attend(joined, places)
    mixed = product(mixed, spread).astype(BF16)
    w_out = w_qo[:, 3 * feat :]
    hidden_one = rows + (product(mixed, w_out) + shifts[3])
    normed_two = norm_rows(hidden_one, gains[1], shifts[4]).astype(BF16)
    normed_two = product(normed_two, spread).astype(BF16)
    inner = product(normed_two, w_up) + up_bias
    active = jax.nn.gelu(inner, approximate=False).astype(BF16)
    result = (hidden_one + (product(active, w_down) + shifts[5])).astype(BF16)
    return result, (rows, normed_one, joined, stats, mixed, w_out, hidden_one, normed_two, inner, active)


def gather_back(values, spread):
    high = lax.reduce_precision(values, 8, 7)
    low = (values - high).astype(BF16)
    return against(high.astype(BF16), spread) + against(low, spread)


def layer_backward(grad_rows, places, weights, state, spread, ship):
    w_qo, w_up, w_down, gains, shifts, up_bias = weights
    rows, normed_one, joined, stats, mixed, w_out, hidden_one, normed_two, inner, active = state
    count, feat = rows.shape
    data_devices = ship.links.count
    down_in = grad_rows
    ship.down(outer_sum(active, down_in).astype(BF16))
    grad_bdown = jnp.sum(down_in, axis=0, dtype=F32)
    d_active = against(down_in, w_down)
    gelu_back = jax.vjp(lambda v: jax.nn.gelu(v, approximate=False), inner)[1]
    d_inner = gelu_back(d_active)[0].astype(BF16)
    ship.up(normed_two, d_inner)
    grad_bup = jnp.sum(d_inner, axis=0, dtype=F32)
    d_second = gather_back(against(d_inner, w_up), spread)
    second_back = jax.vjp(norm_rows, hidden_one, gains[1], shifts[4])[1]
    d_hidden, grad_gain_two, grad_shift_two = second_back(d_second)
    d_hidden = grad_rows.astype(F32) + d_hidden
    out_in = d_hidden.astype(BF16)
    grad_wout = outer_sum(mixed, out_in)
    grad_bout = jnp.sum(out_in, axis=0, dtype=F32)
    d_mixed = against(out_in, w_out).astype(BF16)
    d_mixed = against(d_mixed, spread).astype(BF16)
    d_joined = attend_back(joined, places, stats, d_mixed)
    grad_wqkv = outer_sum(normed_one, d_joined)
    joined_sums = jnp.sum(d_joined, axis=0, dtype=F32)
    w_qkv_grad = jnp.concatenate([d_joined, jnp.zeros((count, feat), BF16)], axis=1)
    d_first = gather_back(against(w_qkv_grad, w_qo), spread)
    first_back = jax.vjp(norm_rows, rows, gains[0], shifts[0])[1]
    d_input, grad_gain_one, grad_shift_one = first_back(d_first)
    d_input = d_hidden + d_input
    small = [
        grad_gain_one,
        grad_gain_two,
        grad_shift_one,
        joined_sums[:feat],
        joined_sums[2 * feat :],
        grad_bout,
        grad_shift_two,
        grad_bdown,
        grad_bup,
    ]
    small = jnp.concatenate([item.reshape(data_devices, -1) for item in small], axis=1)
    ship.attention(grad_wqkv.astype(BF16), grad_wout.astype(BF16), small)
    return d_input


class Shipper:
    def __init__(self, links, own_rows, pad_rows, cols):
        self.links = links
        self.own = own_rows
        self.pad = pad_rows
        self.cols = cols

    def finish(self, keep, away):
        total = (keep.astype(F32) + self.links.swap_cores(away).astype(F32)).astype(BF16)
        return self.links.reduce(total)

    def down(self, grad):
        core = self.links.core
        grad = grad.reshape(self.links.count, 2, -1, grad.shape[1])
        keep = lax.dynamic_slice_in_dim(grad, core, 1, 1)[:, 0]
        away = lax.dynamic_slice_in_dim(grad, 1 - core, 1, 1)[:, 0]
        self.down_done = self.finish(keep, away)

    def up(self, left, right):
        core = self.links.core
        half = self.cols // 2
        shape = (self.links.count, self.pad, half)
        away = outer_sum(left, lax.dynamic_slice_in_dim(right, (1 - core) * half, half, 1))
        keep = outer_sum(left, lax.dynamic_slice_in_dim(right, core * half, half, 1))
        self.up_done = self.finish(
            keep.astype(BF16).reshape(shape), away.astype(BF16).reshape(shape)
        )

    def attention(self, grad_qkv, grad_out, small):
        core = self.links.core
        half = self.cols // 2
        grad = jnp.concatenate([grad_qkv, grad_out], axis=1)
        grad = grad.reshape(self.links.count, self.pad, self.cols)
        small = jnp.pad(small.astype(BF16), ((0, 0), (0, self.cols - small.shape[1])))
        row = lax.broadcasted_iota(jnp.int32, grad.shape, 1)
        grad = jnp.where(row == self.own, small[:, None, :], grad)
        keep = lax.dynamic_slice_in_dim(grad, core * half, half, 2)
        away = lax.dynamic_slice_in_dim(grad, (1 - core) * half, half, 2)
        self.attention_done = self.finish(keep, away)


def per_device(
    tokens, positions, cotangent, w_qkv, w_out, w_up, w_down, norm_gains, biases, up_bias
):
    data_devices = lax.axis_size("dp")
    links = Links(data_devices)
    core = links.core
    own = w_qkv.shape[1]
    pad = (own // 8 + 1) * 8
    feat = own * data_devices
    cols = w_up.shape[2]
    half = cols // 2
    count = tokens.shape[0] // 2

    feature = lax.broadcasted_iota(jnp.int32, (feat, pad * data_devices), 0)
    column = lax.broadcasted_iota(jnp.int32, (feat, pad * data_devices), 1)
    spread = (column == feature // own * pad + feature % own).astype(BF16)

    small = jnp.concatenate([norm_gains[0].reshape(-1), biases[0].reshape(-1), up_bias[0]])
    small_size = small.shape[0]
    small = jnp.pad(small, (0, cols - small_size))[None]
    shard_qo = jnp.concatenate([w_qkv[0], w_out[0]], axis=1)
    shard_qo = jnp.concatenate([shard_qo, small, jnp.zeros((pad - own - 1, cols), BF16)], axis=0)
    shard_up = jnp.pad(w_up[0], ((0, pad - own), (0, 0)))
    shard_down = w_down[0]
    down_half = shard_down.shape[0] // 2

    def own_halves(shard, size, axis):
        keep = lax.dynamic_slice_in_dim(shard, core * size, size, axis)
        away = lax.dynamic_slice_in_dim(shard, (1 - core) * size, size, axis)
        other = links.swap_cores(away)
        return (jnp.where(core == 0, keep, other), jnp.where(core == 0, other, keep))

    halves_qo = own_halves(shard_qo, half, 1)
    halves_up = own_halves(shard_up, half, 1)
    halves_down = own_halves(shard_down, down_half, 0)

    def whole(part, axis):
        other = links.swap_cores(part)
        shape = part.shape[:axis] + (2 * part.shape[axis],) + part.shape[axis + 1 :]
        out = jnp.zeros(shape, part.dtype)
        size = part.shape[axis]
        out = lax.dynamic_update_slice_in_dim(out, part, core * size, axis)
        return lax.dynamic_update_slice_in_dim(out, other, (1 - core) * size, axis)

    layers = []
    for layer in range(2):
        qo = whole(links.gather(halves_qo[layer]), 2)
        up = whole(links.gather(halves_up[layer]), 2)
        down = links.gather(halves_down[layer])
        down = whole(down[:, None], 1).reshape(-1, feat)
        smalls = qo[:, own, :small_size].astype(F32)
        gains = smalls[:, : 2 * own].reshape(data_devices, 2, own)
        gains = gains.transpose(1, 0, 2).reshape(2, feat)
        shifts = smalls[:, 2 * own : 8 * own].reshape(data_devices, 6, own)
        shifts = shifts.transpose(1, 0, 2).reshape(6, feat)
        bias = smalls[:, 8 * own :].reshape(-1)
        layers.append(
            (qo.reshape(-1, cols), up.reshape(-1, cols), down, gains, shifts, bias)
        )

    source = lax.dynamic_slice_in_dim(tokens, core * count, count)
    places = lax.dynamic_slice_in_dim(positions, core * count, count)
    cotan = lax.dynamic_slice_in_dim(cotangent, core * count, count)
    first_out, first_state = layer_forward(source, places, layers[0], spread)
    second_out, second_state = layer_forward(first_out, places, layers[1], spread)
    ships = [Shipper(links, own, pad, cols) for _ in range(2)]
    second_grad = layer_backward(cotan, places, layers[1], second_state, spread, ships[1])
    first_grad = layer_backward(
        second_grad.astype(BF16), places, layers[0], first_state, spread, ships[0]
    )

    def by_layer(first, second):
        mine = jnp.where(core == 0, first, second)
        other = links.swap_cores(jnp.where(core == 0, second, first))
        return jnp.where(core == 0, mine, other), jnp.where(core == 0, other, mine)

    acts = jnp.concatenate(by_layer(first_out, second_out), axis=0)[None]
    grads = jnp.concatenate(by_layer(first_grad, second_grad), axis=0)[None]

    qo = jnp.concatenate(by_layer(ships[0].attention_done, ships[1].attention_done), axis=1)
    up = jnp.concatenate(by_layer(ships[0].up_done, ships[1].up_done), axis=1)
    down = jnp.concatenate(by_layer(ships[0].down_done, ships[1].down_done), axis=0)
    smalls = qo[own, :small_size]
    return (
        acts,
        grads,
        qo[None, :own, : 3 * feat],
        qo[None, :own, 3 * feat :],
        up[None, :own],
        down[None],
        smalls[: 2 * own].reshape(1, 2, own),
        smalls[2 * own : 8 * own].reshape(1, 6, own),
        smalls[8 * own :][None],
    )


def solution(mesh):
    rows = P("dp", None)
    weight = P("section", "dp", None)
    vector = P("section", None, "dp")
    in_specs = (rows, P("dp"), rows, weight, weight, weight, weight, vector, vector, P("section", "dp"))
    out_specs = (weight, weight, weight, weight, weight, weight, vector, vector, P("section", "dp"))
    return jax.shard_map(
        per_device, mesh=mesh, in_specs=in_specs, out_specs=out_specs, check_vma=False
    )
```

time: 3190 us -> 1430 us (0.45)
  waiting for transfers between devices: 2090 us -> 460 us
  blocking collectives: 242 us -> 0 us
  starting transfers between devices: 9 us -> 161 us
  local copies, waits for them, and re-layouts: 203 us -> 249 us
  other arithmetic: 201 us -> 168 us
    unnamed x14 -> x0, waiting for transfers between devices: 1470 us -> none
    all_gather x4 -> x0, waiting for transfers between devices: 409 us -> none  [the longest x1 204 us: per_device(): lax.all_gather(w_up, 'dp', axis=1, tiled=True)]
    ppermute x4 -> x80, waiting for transfers between devices: 214 us -> 460 us  [send(): return lax.ppermute(x, BOTH, perm)]
    ppermute x4 -> x80, starting transfers between devices: 8.63 us -> 161 us  [send(): return lax.ppermute(x, BOTH, perm)]
    all_gather x2 -> x0, blocking collectives: 91.6 us -> none  [the longest x1 49.2 us: per_device(): lax.all_gather(norm_gains, 'dp', axis=2, tiled=True)]
    broadcast_in_dim x5 -> x3, local copies, waits for them, and re-layouts: 89.6 us -> 0.16 us  [the longest x1 0.14 us: per_device(): qo[None, :own, 3 * feat:]]
    dynamic_update_slice x0 -> x35, local copies, waits for them, and re-layouts: none -> 82.1 us  [the longest x23 29.7 us: gather(): out = lax.dynamic_update_slice_in_dim(out, part[:, None], place, 1)]
    squeeze x1 -> x0, blocking collectives: 75.6 us -> none  [per_device(): layer_weights = tuple((item[0] for item in gathered))]
  transfers between devices with their start and end apart: 13 -> 80, of which waited for: 10 -> 27; matrix products, arithmetic and copies ran while one was open for 7% -> 33% of each run, Pallas kernels for 0% -> 0%
where the time goes in v1:
time: 1430 us
  waiting for transfers between devices  460 us (32%)
  matrix products  385 us (27%)
  local copies, waits for them, and re-layouts  249 us (17%)
  other arithmetic  168 us (12%)
  starting transfers between devices  161 us (11%)
    ppermute x80, waiting for transfers between devices, send(): return lax.ppermute(x, BOTH, perm)  460 us
    ppermute x80, starting transfers between devices, send(): return lax.ppermute(x, BOTH, perm)  161 us
    dot_general x14, matrix products, product(): return jnp.dot(left, right, preferred_element_type=F32)  123 us
    dot_general x16, matrix products, against(): lax.dot_general(left, right, (((1,), (1,)), ((), ())), preferred_element_...  105 us
    dot_general x10, matrix products, outer_sum(): lax.dot_general(left, right, (((0,), (0,)), ((), ())), preferred_element_...  65.9 us
    convert_element_type x6, other arithmetic, finish(): (keep.astype(F32) + self.links.swap_cores(away).astype(F32)).astype(BF16)  34.1 us
    another operation x13, local copies, waits for them, and re-layouts  33.3 us
    unnamed x309, local copies, waits for them, and re-layouts  32.4 us
  transfers between devices with their start and end apart: 80, of which 27 were waited for; matrix products, arithmetic and copies ran while one was open for 33% of the time, Pallas kernels for 0%

profile of v1, /device:TPU:0, one launch (start us, length us, event | category | flops | bytes accessed | tf_op | source)
XLA Modules:
  0.0 1426.5 jit_solution(2129434003018961428)
XLA Ops:
  38.0 16.7 %collective-permute-start.17 = (bf16[136,1088]{1,0:T(8,128)(2,1)S(1)}, bf16[136,1088]{1,0:T(8,128)(2,1)S(1)}, u32[]{:S(2)}, u32[]{:S(2)}) collective-permute-start(bf16[136,1088]{1,0:T(8,128)(2,1)S(1)} %get-tuple-element.151), channel_id=1, source_target_pairs={{0,4},{1,5},{2,6},{3,7},{4,8},{5,9},{6,10},{7,11},{8,12},{9,13},{1... | collective-permute-start | bytes 887816 | tf_op jit(solution)/shard_map/ppermute | solution.py:67
  63.4 17.3 %collective-permute-done.16 = bf16[136,1088]{1,0:T(8,128)(2,1)S(1)} collective-permute-done((bf16[136,1088]{1,0:T(8,128)(2,1)S(1)}, bf16[136,1088]{1,0:T(8,128)(2,1)S(1)}, u32[]{:S(2)}, u32[]{:S(2)}) %collective-permute-start.16) | collective-permute-done | bytes 295968 | tf_op jit(solution)/shard_map/ppermute | solution.py:67
  117.2 17.3 %collective-permute-done.2 = bf16[72,2176]{1,0:T(8,128)(2,1)S(1)} collective-permute-done((bf16[72,2176]{1,0:T(8,128)(2,1)S(1)}, bf16[72,2176]{1,0:T(8,128)(2,1)S(1)}, u32[]{:S(2)}, u32[]{:S(2)}) %collective-permute-start.2) | collective-permute-done | bytes 313376 | tf_op jit(solution)/shard_map/ppermute | solution.py:67
  199.4 14.7 %collective-permute-done.4 = bf16[4,72,2176]{2,1,0:T(8,128)(2,1)S(1)} collective-permute-done((bf16[4,72,2176]{2,1,0:T(8,128)(2,1)S(1)}, bf16[4,72,2176]{2,1,0:T(8,128)(2,1)S(1)}, u32[]{:S(2)}, u32[]{:S(2)}) %collective-permute-start.4) | collective-permute-done | bytes 1253408 | tf_op jit(solution)/shard_map/ppermute | solution.py:67
  218.4 22.5 %collective-permute-done.24 = bf16[4,72,2176]{2,1,0:T(8,128)(2,1)S(1)} collective-permute-done((bf16[4,72,2176]{2,1,0:T(8,128)(2,1)S(1)}, bf16[4,72,2176]{2,1,0:T(8,128)(2,1)S(1)}, u32[]{:S(2)}, u32[]{:S(2)}) %collective-permute-start.24) | collective-permute-done | bytes 1253408 | tf_op jit(solution)/shard_map/ppermute | solution.py:67
  245.3 49.3 %collective-permute-done.30 = bf16[4,72,2176]{2,1,0:T(8,128)(2,1)S(1)} collective-permute-done((bf16[4,72,2176]{2,1,0:T(8,128)(2,1)S(1)}, bf16[4,72,2176]{2,1,0:T(8,128)(2,1)S(1)}, u32[]{:S(2)}, u32[]{:S(2)}) %collective-permute-start.30) | collective-permute-done | bytes 1253408 | tf_op jit(solution)/shard_map/ppermute | solution.py:67
  322.5 30.8 %collective-permute-done.25 = bf16[2,4,72,2176]{3,2,1,0:T(8,128)(2,1)} collective-permute-done((bf16[2,4,72,2176]{3,2,1,0:T(8,128)(2,1)}, bf16[2,4,72,2176]{3,2,1,0:T(8,128)(2,1)}, u32[]{:S(2)}, u32[]{:S(2)}) %collective-permute-start.25) | collective-permute-done | bytes 2506784 | tf_op jit(solution)/shard_map/ppermute | solution.py:67
  362.5 17.7 %collective-permute-done.31 = bf16[2,4,72,2176]{3,2,1,0:T(8,128)(2,1)} collective-permute-done((bf16[2,4,72,2176]{3,2,1,0:T(8,128)(2,1)}, bf16[2,4,72,2176]{3,2,1,0:T(8,128)(2,1)}, u32[]{:S(2)}, u32[]{:S(2)}) %collective-permute-start.31) | collective-permute-done | bytes 2506784 | tf_op jit(solution)/shard_map/ppermute | solution.py:67
  381.5 25.5 %collective-permute-done.12 = bf16[2,4,72,2176]{3,2,1,0:T(8,128)(2,1)} collective-permute-done((bf16[2,4,72,2176]{3,2,1,0:T(8,128)(2,1)}, bf16[2,4,72,2176]{3,2,1,0:T(8,128)(2,1)}, u32[]{:S(2)}, u32[]{:S(2)}) %collective-permute-start.12) | collective-permute-done | bytes 2506784 | tf_op jit(solution)/shard_map/ppermute | solution.py:67
  527.5 27.5 %multiply_convert_fusion.3 = (bf16[512,4352]{1,0:T(8,128)(2,1)}, f32[512,4352]{1,0:T(8,128)}, f32[512,4352]{1,0:T(8,128)}) fusion(f32[4352]{0:T(1024)S(1)} %add.637, bf16[512,1152]{1,0:T(8,128)(2,1)S(1)} %convolution_convert_fusion.17, bf16[1152,4352]{1,0:T(8,128)(2,1)S(1)} %bitcast.674), kind=kOutput, calls=%fused_computation.56 | convolution fusion | flops 5280890880 | bytes 33506304 | tf_op jit(solution)/shard_map/dot_general | solution.py:28
  611.6 27.6 %multiply_convert_fusion.2 = (bf16[512,4352]{1,0:T(8,128)(2,1)}, f32[512,4352]{1,0:T(8,128)}, f32[512,4352]{1,0:T(8,128)}) fusion(f32[4352]{0:T(1024)S(1)} %copy-done.59, bf16[512,1152]{1,0:T(8,128)(2,1)S(1)} %convolution_convert_fusion.14, bf16[1152,4352]{1,0:T(8,128)(2,1)S(1)} %bitcast.678), kind=kOutput, calls=%fused_computation.42 | convolution fusion | flops 5280890880 | bytes 33506304 | tf_op jit(solution)/shard_map/dot_general | solution.py:28
  639.2 15.4 %fusion.250 = (bf16[4352]{0:T(1024)(128)(2,1)}, bf16[512,4352]{1,0:T(8,128)(2,1)}) fusion(f32[512,4352]{1,0:T(8,128)} %get-tuple-element.85, bf16[4352,1088]{1,0:T(8,128)(2,1)} %bitcast.670, bf16[1024,1088]{0,1:T(8,128)(2,1)S(1)} %copy-done.38, s32[]{:T(128)S(6)} %select_n.424, f32[512,4352]{1,0:T(8,128)} %get-tuple-element.173, f32[4352]{0:T(1024)S(1)} %copy-done.59), kind=kOutput, calls=%fused_computation.577 | convolution fusion | flops 4884262912 | bytes 32895492 | tf_op jit(solution)/shard_map/dot_general | solution.py:36
  762.3 15.6 %convert_reduce_fusion.2 = (bf16[1088]{0:T(1024)(128)(2,1)}, f32[512,1088]{0,1:T(8,128)S(1)}, bf16[1088]{0:T(1024)(128)(2,1)}, bf16[512,1088]{0,1:T(8,128)(2,1)}, bf16[512,1088]{0,1:T(8,128)(2,1)}) fusion(f32[512]{0:T(512)S(1)} %negate_multiply_fusion.4, f32[512]{0:T(512)S(1)} %multiply_multiply_fusion.12, f32[512]{0:T(512)S(1)} %copy-done.63, ...), kind=kOutput, calls=%fused_computation.345 | convolution fusion | flops 4859197440 | bytes 27319044 | tf_op jit(solution)/shard_map/dot_general | solution.py:28
  777.9 15.6 %fusion.251 = (bf16[4352]{0:T(1024)(128)(2,1)S(1)}, bf16[512,4352]{1,0:T(8,128)(2,1)}) fusion(f32[512,4352]{1,0:T(8,128)} %get-tuple-element.99, bf16[4352,1088]{1,0:T(8,128)(2,1)} %bitcast.666, f32[512,1088]{0,1:T(8,128)S(1)} %get-tuple-element.67, f32[512,4352]{1,0:T(8,128)} %get-tuple-element.166, f32[4352]{0:T(1024)S(1)} %copy-done.58), kind=kOutput, calls=%fused_computation.578 | convolution fusion | flops 4884819968 | bytes 34006528 | tf_op jit(solution)/shard_map/dot_general | solution.py:36
  899.9 13.9 copy.120
  935.3 14.1 copy.110
  949.4 13.9 copy.117
  984.0 13.6 pad_maximum_fusion
  997.6 14.1 copy.107
  1121.8 36.9 %collective-permute-done.61 = bf16[2,4,72,2176]{3,2,1,0:T(8,128)(2,1)} collective-permute-done((bf16[2,4,72,2176]{3,2,1,0:T(8,128)(2,1)}, bf16[2,4,72,2176]{3,2,1,0:T(8,128)(2,1)}, u32[]{:S(2)}, u32[]{:S(2)}) %collective-permute-start.61) | collective-permute-done | bytes 2506784 | tf_op jit(solution)/shard_map/ppermute | solution.py:67
  1161.8 37.2 %collective-permute-done.55 = bf16[2,4,72,2176]{3,2,1,0:T(8,128)(2,1)} collective-permute-done((bf16[2,4,72,2176]{3,2,1,0:T(8,128)(2,1)}, bf16[2,4,72,2176]{3,2,1,0:T(8,128)(2,1)}, u32[]{:S(2)}, u32[]{:S(2)}) %collective-permute-start.55) | collective-permute-done | bytes 2506784 | tf_op jit(solution)/shard_map/ppermute | solution.py:67
  1202.1 37.2 %collective-permute-done.42 = bf16[2,4,72,2176]{3,2,1,0:T(8,128)(2,1)} collective-permute-done((bf16[2,4,72,2176]{3,2,1,0:T(8,128)(2,1)}, bf16[2,4,72,2176]{3,2,1,0:T(8,128)(2,1)}, u32[]{:S(2)}, u32[]{:S(2)}) %collective-permute-start.42) | collective-permute-done | bytes 2506784 | tf_op jit(solution)/shard_map/ppermute | solution.py:67
  1364.1 19.6 %collective-permute-done.58 = bf16[72,2176]{1,0:T(8,128)(2,1)S(1)} collective-permute-done((bf16[72,2176]{1,0:T(8,128)(2,1)S(1)}, bf16[72,2176]{1,0:T(8,128)(2,1)S(1)}, u32[]{:S(2)}, u32[]{:S(2)}) %collective-permute-start.58) | collective-permute-done | bytes 313376 | tf_op jit(solution)/shard_map/ppermute | solution.py:67
  1384.1 19.7 %collective-permute-done.45 = bf16[72,2176]{1,0:T(8,128)(2,1)S(1)} collective-permute-done((bf16[72,2176]{1,0:T(8,128)(2,1)S(1)}, bf16[72,2176]{1,0:T(8,128)(2,1)S(1)}, u32[]{:S(2)}, u32[]{:S(2)}) %collective-permute-start.45) | collective-permute-done | bytes 313376 | tf_op jit(solution)/shard_map/ppermute | solution.py:67
  (746 shorter events, 889.6 us)
Async XLA Ops:
  174.8 66.1 %collective-permute-start.24 = (bf16[4,72,2176]{2,1,0:T(8,128)(2,1)S(1)}, bf16[4,72,2176]{2,1,0:T(8,128)(2,1)S(1)}, u32[]{:S(2)}, u32[]{:S(2)}) collective-permute-start(bf16[4,72,2176]{2,1,0:T(8,128)(2,1)S(1)} %get-tuple-element.91), channel_id=1, source_target_pairs={{0,1},{1,0},{2,3},{3,2},{4,5},{5,4},{6,7},{7,6},{8,9},{9,8},{10,11... | collective-permute-start | bytes 3760136 | tf_op jit(solution)/shard_map/ppermute | solution.py:67
  186.0 112.9 %collective-permute-start.11 = (bf16[4,72,2176]{2,1,0:T(8,128)(2,1)S(1)}, bf16[4,72,2176]{2,1,0:T(8,128)(2,1)S(1)}, u32[]{:S(2)}, u32[]{:S(2)}) collective-permute-start(bf16[4,72,2176]{2,1,0:T(8,128)(2,1)S(1)} %get-tuple-element.101), channel_id=1, source_target_pairs={{0,1},{1,0},{2,3},{3,2},{4,5},{5,4},{6,7},{7,6},{8,9},{9,8},{10,11... | collective-permute-start | bytes 3760136 | tf_op jit(solution)/shard_map/ppermute | solution.py:67
  193.9 100.7 %collective-permute-start.30 = (bf16[4,72,2176]{2,1,0:T(8,128)(2,1)S(1)}, bf16[4,72,2176]{2,1,0:T(8,128)(2,1)S(1)}, u32[]{:S(2)}, u32[]{:S(2)}) collective-permute-start(bf16[4,72,2176]{2,1,0:T(8,128)(2,1)S(1)} %get-tuple-element.87), channel_id=1, source_target_pairs={{0,1},{1,0},{2,3},{3,2},{4,5},{5,4},{6,7},{7,6},{8,9},{9,8},{10,11... | collective-permute-start | bytes 3760136 | tf_op jit(solution)/shard_map/ppermute | solution.py:67
  197.4 115.1 %collective-permute-start.37 = (bf16[2,4,136,1088]{3,2,1,0:T(8,128)(2,1)}, bf16[2,4,136,1088]{3,2,1,0:T(8,128)(2,1)}, u32[]{:S(2)}, u32[]{:S(2)}) collective-permute-start(bf16[2,4,136,1088]{3,2,1,0:T(8,128)(2,1)} %pad_maximum_fusion.7), channel_id=1, source_target_pairs={{0,2},{1,3},{2,0},{3,1},{4,6},{5,7},{6,4},{7,5},{8,10},{9,11},{10,... | collective-permute-start | bytes 7102472 | tf_op jit(solution)/shard_map/ppermute | solution.py:67
  214.1 88.9 %collective-permute-start.19 = (bf16[2,4,136,1088]{3,2,1,0:T(8,128)(2,1)S(1)}, bf16[2,4,136,1088]{3,2,1,0:T(8,128)(2,1)S(1)}, u32[]{:S(2)}, u32[]{:S(2)}) collective-permute-start(bf16[2,4,136,1088]{3,2,1,0:T(8,128)(2,1)S(1)} %pad_maximum_fusion.4), channel_id=1, source_target_pairs={{0,2},{1,3},{2,0},{3,1},{4,6},{5,7},{6,4},{7,5},{8,10},{9,11},{10,... | collective-permute-start | bytes 7102472 | tf_op jit(solution)/shard_map/ppermute | solution.py:67
  240.9 118.6 %collective-permute-start.5 = (bf16[2,4,72,2176]{3,2,1,0:T(8,128)(2,1)}, bf16[2,4,72,2176]{3,2,1,0:T(8,128)(2,1)}, u32[]{:S(2)}, u32[]{:S(2)}) collective-permute-start(bf16[2,4,72,2176]{3,2,1,0:T(8,128)(2,1)} %pad_maximum_fusion.2), channel_id=1, source_target_pairs={{0,2},{1,3},{2,0},{3,1},{4,6},{5,7},{6,4},{7,5},{8,10},{9,11},{10,... | collective-permute-start | bytes 7520264 | tf_op jit(solution)/shard_map/ppermute | solution.py:67
  298.9 81.3 %collective-permute-start.31 = (bf16[2,4,72,2176]{3,2,1,0:T(8,128)(2,1)}, bf16[2,4,72,2176]{3,2,1,0:T(8,128)(2,1)}, u32[]{:S(2)}, u32[]{:S(2)}) collective-permute-start(bf16[2,4,72,2176]{3,2,1,0:T(8,128)(2,1)} %pad_maximum_fusion.6), channel_id=1, source_target_pairs={{0,2},{1,3},{2,0},{3,1},{4,6},{5,7},{6,4},{7,5},{8,10},{9,11},{10,... | collective-permute-start | bytes 7520264 | tf_op jit(solution)/shard_map/ppermute | solution.py:67
  302.9 104.1 %collective-permute-start.12 = (bf16[2,4,72,2176]{3,2,1,0:T(8,128)(2,1)}, bf16[2,4,72,2176]{3,2,1,0:T(8,128)(2,1)}, u32[]{:S(2)}, u32[]{:S(2)}) collective-permute-start(bf16[2,4,72,2176]{3,2,1,0:T(8,128)(2,1)} %pad_maximum_fusion.3), channel_id=1, source_target_pairs={{0,2},{1,3},{2,0},{3,1},{4,6},{5,7},{6,4},{7,5},{8,10},{9,11},{10,... | collective-permute-start | bytes 7520264 | tf_op jit(solution)/shard_map/ppermute | solution.py:67
  312.5 139.9 %collective-permute-start.20 = (bf16[16,1,136,1088]{3,2,0,1:T(8,128)(2,1)S(1)}, bf16[16,1,136,1088]{3,2,0,1:T(8,128)(2,1)}, u32[]{:S(2)}, u32[]{:S(2)}) collective-permute-start(bf16[16,1,136,1088]{3,2,0,1:T(8,128)(2,1)S(1)} %bitcast.629), channel_id=1, source_target_pairs={{0,16},{1,17},{2,18},{3,19},{4,20},{5,21},{6,22},{7,23},{8,24},{9,... | collective-permute-start | bytes 14204936 | tf_op jit(solution)/shard_map/ppermute | solution.py:67
  353.3 104.6 %collective-permute-start.38 = (bf16[16,1,136,1088]{3,2,0,1:T(8,128)(2,1)S(1)}, bf16[16,1,136,1088]{3,2,0,1:T(8,128)(2,1)}, u32[]{:S(2)}, u32[]{:S(2)}) collective-permute-start(bf16[16,1,136,1088]{3,2,0,1:T(8,128)(2,1)S(1)} %bitcast.627), channel_id=1, source_target_pairs={{0,16},{1,17},{2,18},{3,19},{4,20},{5,21},{6,22},{7,23},{8,24},{9,... | collective-permute-start | bytes 14204936 | tf_op jit(solution)/shard_map/ppermute | solution.py:67
  359.5 108.2 %collective-permute-start.26 = (bf16[16,72,2176]{2,1,0:T(8,128)(2,1)}, bf16[16,72,2176]{2,1,0:T(8,128)(2,1)}, u32[]{:S(2)}, u32[]{:S(2)}) collective-permute-start(bf16[16,72,2176]{2,1,0:T(8,128)(2,1)} %bitcast.632), channel_id=1, source_target_pairs={{0,16},{1,17},{2,18},{3,19},{4,20},{5,21},{6,22},{7,23},{8,24},{9,... | collective-permute-start | bytes 15040520 | tf_op jit(solution)/shard_map/ppermute | solution.py:67
  380.2 83.4 %collective-permute-start.6 = (bf16[16,72,2176]{2,1,0:T(8,128)(2,1)S(1)}, bf16[16,72,2176]{2,1,0:T(8,128)(2,1)}, u32[]{:S(2)}, u32[]{:S(2)}) collective-permute-start(bf16[16,72,2176]{2,1,0:T(8,128)(2,1)S(1)} %bitcast.630), channel_id=1, source_target_pairs={{0,16},{1,17},{2,18},{3,19},{4,20},{5,21},{6,22},{7,23},{8,24},{9,... | collective-permute-start | bytes 15040520 | tf_op jit(solution)/shard_map/ppermute | solution.py:67
  412.8 111.1 %collective-permute-start.13 = (bf16[16,72,2176]{2,1,0:T(8,128)(2,1)}, bf16[16,72,2176]{2,1,0:T(8,128)(2,1)}, u32[]{:S(2)}, u32[]{:S(2)}) collective-permute-start(bf16[16,72,2176]{2,1,0:T(8,128)(2,1)} %bitcast.38), channel_id=1, source_target_pairs={{0,16},{1,17},{2,18},{3,19},{4,20},{5,21},{6,22},{7,23},{8,24},{9,... | collective-permute-start | bytes 15040520 | tf_op jit(solution)/shard_map/ppermute | solution.py:67
  452.4 155.6 %collective-permute-start.32 = (bf16[16,72,2176]{2,1,0:T(8,128)(2,1)}, bf16[16,72,2176]{2,1,0:T(8,128)(2,1)}, u32[]{:S(2)}, u32[]{:S(2)}) collective-permute-start(bf16[16,72,2176]{2,1,0:T(8,128)(2,1)} %bitcast.94), channel_id=1, source_target_pairs={{0,16},{1,17},{2,18},{3,19},{4,20},{5,21},{6,22},{7,23},{8,24},{9,... | collective-permute-start | bytes 15040520 | tf_op jit(solution)/shard_map/ppermute | solution.py:67
  918.9 132.2 %collective-permute-start.73 = (bf16[16,136,1088]{2,1,0:T(8,128)(2,1)}, bf16[16,136,1088]{2,1,0:T(8,128)(2,1)}, u32[]{:S(2)}, u32[]{:S(2)}) collective-permute-start(bf16[16,136,1088]{2,1,0:T(8,128)(2,1)} %dynamic-slice_bitcast_fusion), channel_id=1, source_target_pairs={{0,16},{1,17},{2,18},{3,19},{4,20},{5,21},{6,22},{7,23},{8,24},{9,... | collective-permute-start | bytes 14204936 | tf_op jit(solution)/shard_map/ppermute | solution.py:67
  920.3 121.6 %collective-permute-start.39 = (bf16[512,1088]{0,1:T(8,128)(2,1)}, bf16[512,1088]{0,1:T(8,128)(2,1)S(1)}, u32[]{:S(2)}, u32[]{:S(2)}) collective-permute-start(bf16[512,1088]{0,1:T(8,128)(2,1)} %get-tuple-element.149), channel_id=1, source_target_pairs={{0,16},{1,17},{2,18},{3,19},{4,20},{5,21},{6,22},{7,23},{8,24},{9,... | collective-permute-start | bytes 3342344 | tf_op jit(solution)/shard_map/ppermute | solution.py:67
  1081.2 77.5 %collective-permute-start.61 = (bf16[2,4,72,2176]{3,2,1,0:T(8,128)(2,1)}, bf16[2,4,72,2176]{3,2,1,0:T(8,128)(2,1)}, u32[]{:S(2)}, u32[]{:S(2)}) collective-permute-start(bf16[2,4,72,2176]{3,2,1,0:T(8,128)(2,1)} %pad_maximum_fusion.11), channel_id=1, source_target_pairs={{0,2},{1,3},{2,0},{3,1},{4,6},{5,7},{6,4},{7,5},{8,10},{9,11},{10,... | collective-permute-start | bytes 7520264 | tf_op jit(solution)/shard_map/ppermute | solution.py:67
  1090.0 109.0 %collective-permute-start.55 = (bf16[2,4,72,2176]{3,2,1,0:T(8,128)(2,1)}, bf16[2,4,72,2176]{3,2,1,0:T(8,128)(2,1)}, u32[]{:S(2)}, u32[]{:S(2)}) collective-permute-start(bf16[2,4,72,2176]{3,2,1,0:T(8,128)(2,1)} %pad_maximum_fusion.10), channel_id=1, source_target_pairs={{0,2},{1,3},{2,0},{3,1},{4,6},{5,7},{6,4},{7,5},{8,10},{9,11},{10,... | collective-permute-start | bytes 7520264 | tf_op jit(solution)/shard_map/ppermute | solution.py:67
  1101.5 137.8 %collective-permute-start.42 = (bf16[2,4,72,2176]{3,2,1,0:T(8,128)(2,1)}, bf16[2,4,72,2176]{3,2,1,0:T(8,128)(2,1)}, u32[]{:S(2)}, u32[]{:S(2)}) collective-permute-start(bf16[2,4,72,2176]{3,2,1,0:T(8,128)(2,1)} %pad_maximum_fusion.8), channel_id=1, source_target_pairs={{0,2},{1,3},{2,0},{3,1},{4,6},{5,7},{6,4},{7,5},{8,10},{9,11},{10,... | collective-permute-start | bytes 7520264 | tf_op jit(solution)/shard_map/ppermute | solution.py:67
  1111.4 154.7 %collective-permute-start.48 = (bf16[2,4,72,2176]{3,2,1,0:T(8,128)(2,1)S(1)}, bf16[2,4,72,2176]{3,2,1,0:T(8,128)(2,1)S(1)}, u32[]{:S(2)}, u32[]{:S(2)}) collective-permute-start(bf16[2,4,72,2176]{3,2,1,0:T(8,128)(2,1)S(1)} %pad_maximum_fusion.9), channel_id=1, source_target_pairs={{0,2},{1,3},{2,0},{3,1},{4,6},{5,7},{6,4},{7,5},{8,10},{9,11},{10,... | collective-permute-start | bytes 7520264 | tf_op jit(solution)/shard_map/ppermute | solution.py:67
  1118.4 122.7 %collective-permute-start.75 = (bf16[4,136,1088]{2,1,0:T(8,128)(2,1)S(1)}, bf16[4,136,1088]{2,1,0:T(8,128)(2,1)S(1)}, u32[]{:S(2)}, u32[]{:S(2)}) collective-permute-start(bf16[4,136,1088]{2,1,0:T(8,128)(2,1)S(1)} %fusion.68), channel_id=1, source_target_pairs={{0,1},{1,0},{2,3},{3,2},{4,5},{5,4},{6,7},{7,6},{8,9},{9,8},{10,11... | collective-permute-start | bytes 3551240 | tf_op jit(solution)/shard_map/ppermute | solution.py:67
  1158.7 92.0 %collective-permute-start.69 = (bf16[4,136,1088]{2,1,0:T(8,128)(2,1)S(1)}, bf16[4,136,1088]{2,1,0:T(8,128)(2,1)S(1)}, u32[]{:S(2)}, u32[]{:S(2)}) collective-permute-start(bf16[4,136,1088]{2,1,0:T(8,128)(2,1)S(1)} %fusion.71), channel_id=1, source_target_pairs={{0,1},{1,0},{2,3},{3,2},{4,5},{5,4},{6,7},{7,6},{8,9},{9,8},{10,11... | collective-permute-start | bytes 3551240 | tf_op jit(solution)/shard_map/ppermute | solution.py:67
  1199.0 105.7 %collective-permute-start.62 = (bf16[4,72,2176]{2,1,0:T(8,128)(2,1)S(1)}, bf16[4,72,2176]{2,1,0:T(8,128)(2,1)S(1)}, u32[]{:S(2)}, u32[]{:S(2)}) collective-permute-start(bf16[4,72,2176]{2,1,0:T(8,128)(2,1)S(1)} %fusion.74), channel_id=1, source_target_pairs={{0,1},{1,0},{2,3},{3,2},{4,5},{5,4},{6,7},{7,6},{8,9},{9,8},{10,11... | collective-permute-start | bytes 3760136 | tf_op jit(solution)/shard_map/ppermute | solution.py:67
  1343.4 60.4 %collective-permute-start.45 = (bf16[72,2176]{1,0:T(8,128)(2,1)S(1)}, bf16[72,2176]{1,0:T(8,128)(2,1)S(1)}, u32[]{:S(2)}, u32[]{:S(2)}) collective-permute-start(bf16[72,2176]{1,0:T(8,128)(2,1)S(1)} %get-tuple-element.148), channel_id=1, source_target_pairs={{0,8},{1,9},{2,10},{3,11},{4,12},{5,13},{6,14},{7,15},{8,0},{9,1},... | collective-permute-start | bytes 940040 | tf_op jit(solution)/shard_map/ppermute | solution.py:67
  (190 other events, 6332.6 us)

commit v2 on v1

v2 whole, which is shorter than its diff:
```python
import jax
import jax.numpy as jnp
from jax import lax
from jax.sharding import PartitionSpec as P

HEAD_DIM = 64
EPSILON = 1e-05
BOTH = ("section", "dp")
F32 = jnp.float32
BF16 = jnp.bfloat16


def norm_rows(values, gain_row, shift_row):
    row_mean = jnp.mean(values, axis=-1, keepdims=True)
    centred = values - row_mean
    row_var = jnp.mean(centred * centred, axis=-1, keepdims=True)
    return centred * lax.rsqrt(row_var + EPSILON) * gain_row + shift_row


def permitted(places):
    count = places.shape[0]
    query_idx = jnp.arange(count, dtype=jnp.int32)[:, None]
    key_idx = jnp.arange(count, dtype=jnp.int32)[None, :]
    return (key_idx <= query_idx) & (key_idx >= query_idx - places[:, None])


def product(left, right):
    return jnp.dot(left, right, preferred_element_type=F32)


def outer_sum(left, right):
    return lax.dot_general(left, right, (((0,), (0,)), ((), ())), preferred_element_type=F32)


def against(left, right):
    return lax.dot_general(left, right, (((1,), (1,)), ((), ())), preferred_element_type=F32)


class Links:
    def __init__(self, data_devices):
        self.count = data_devices
        self.core = lax.axis_index("section")
        self.me = lax.axis_index("dp")
        self.deep = data_devices // 4
        self.staged = data_devices == 16
        self.quad = self.me % 4
        self.level = self.me // 4
        count = data_devices
        index = [(c, d) for c in range(2) for d in range(count)]

        def pairs(move):
            return [(c * count + d, move(c, d)) for c, d in index]

        self.swap = pairs(lambda c, d: (1 - c) * count + d)
        self.first = pairs(lambda c, d: c * count + (d ^ (2 if c == 0 else 1)))
        self.second = pairs(lambda c, d: c * count + (d ^ (1 if c == 0 else 2)))
        self.turns = [
            pairs(lambda c, d, k=k: c * count + (d + 4 * k) % count) for k in range(self.deep)
        ]

    def send(self, x, perm):
        return lax.ppermute(x, BOTH, perm)

    def swap_cores(self, x):
        return self.send(x, self.swap)

    def flips(self, core):
        first = jnp.where(core == 0, 2, 1)
        return [0, 3 - first, first, 3]

    def order(self, core):
        if not self.staged:
            return jnp.arange(self.count)
        quads = self.quad ^ jnp.stack([jnp.int32(v) for v in self.flips(core)])
        levels = (self.level - jnp.arange(self.deep)) % self.deep
        return (levels[None, :] * 4 + quads[:, None]).reshape(-1)


class Gather:
    def __init__(self, links, half, sorted_blocks):
        self.links = links
        self.sorted = sorted_blocks
        self.shape = half.shape
        self.live = [half]

    def stage_turn(self):
        links, (half,) = self.links, self.live
        if not links.staged:
            return
        deep = links.deep
        turned = [half] + [links.send(half, links.turns[k]) for k in range(1, deep)]
        if self.sorted:
            listed = jnp.stack([turned[(-t) % deep] for t in range(2 * deep)])
            self.live = [lax.dynamic_slice_in_dim(listed, deep - links.level, deep, 0)]
        else:
            self.live = [jnp.stack(turned)]

    def stage_second(self):
        if self.links.staged:
            (mine,) = self.live
            self.live = [jnp.stack([mine, self.links.send(mine, self.links.second)])]

    def stage_first(self):
        links = self.links
        if not links.staged:
            self.live = [lax.all_gather(self.live[0], "dp", axis=0)]
            return
        (pair,) = self.live
        parts = [pair, links.send(pair, links.first)]
        if not self.sorted:
            self.live = [jnp.concatenate(parts, axis=0)]
            return
        out = jnp.zeros((links.deep, 4) + self.shape, pair.dtype)
        for place, flip in enumerate(links.flips(links.core)):
            part = parts[place // 2][place % 2]
            out = lax.dynamic_update_slice_in_dim(out, part[:, None], links.quad ^ flip, 1)
        self.live = [out]

    def stage_swap(self):
        (mine,) = self.live
        mine = mine.reshape(-1, self.shape[1])
        self.mine, self.other = mine, self.links.swap_cores(mine)
        self.live = []


class Reduce:
    def __init__(self, links, keep, away, sorted_blocks):
        self.links = links
        self.sorted = sorted_blocks
        shape = (links.count, -1, keep.shape[1])
        self.live = [keep.reshape(shape), away.reshape(shape)]

    def stage_swap(self):
        keep, away = self.live
        total = (keep.astype(F32) + self.links.swap_cores(away).astype(F32)).astype(BF16)
        self.live = [total]

    def stage_first(self):
        links, (total,) = self.links, self.live
        if not links.staged:
            self.live = [lax.psum_scatter(total.astype(F32), "dp", scatter_dimension=0)]
            return
        shape = total.shape[1:]
        if self.sorted:
            quads = total.reshape((links.deep, 4) + shape)
            kept, passed, one, two = [
                lax.dynamic_slice_in_dim(quads, links.quad ^ flip, 1, 1)[:, 0]
                for flip in links.flips(links.core)
            ]
            away = jnp.stack([one, two])
        else:
            quads = total.reshape((4, links.deep) + shape)
            kept, passed, away = quads[0], quads[1], quads[2:]
        arrived = links.send(away, links.first)
        passed = (passed.astype(F32) + arrived[1].astype(F32)).astype(BF16)
        kept = (kept.astype(F32) + arrived[0].astype(F32)).astype(BF16)
        self.live = [kept, passed]

    def stage_second(self):
        if self.links.staged:
            kept, passed = self.live
            arrived = self.links.send(passed, self.links.second)
            self.live = [(kept.astype(F32) + arrived.astype(F32)).astype(BF16)]

    def stage_turn(self):
        links, (kept,) = self.links, self.live
        if links.staged:
            deep = links.deep

            def block(step):
                if not self.sorted:
                    return kept[step]
                place = (links.level + deep - step) % deep
                return lax.dynamic_slice_in_dim(kept, place, 1, 0)[0]

            result = block(0).astype(F32)
            for k in range(1, deep):
                result = result + links.send(block(k), links.turns[deep - k]).astype(F32)
            self.live = [result]


def fence(jobs, others):
    held = lax.optimization_barrier(([job.live for job in jobs], others))
    for job, live in zip(jobs, held[0]):
        job.live = live
    return held[1]


def masked_scores(heads_qkv, places):
    scores = jnp.einsum(
        "qhd,khd->hqk", heads_qkv[:, 0], heads_qkv[:, 1], preferred_element_type=F32
    ) * HEAD_DIM ** (-0.5)
    return jnp.where(permitted(places)[None], scores, -jnp.inf)


def attend(joined, places):
    count, wide = joined.shape
    heads_qkv = joined.reshape(count, 3, -1, HEAD_DIM)
    masked = masked_scores(heads_qkv, places)
    row_top = jnp.max(masked, axis=-1, keepdims=True)
    expo_vals = jnp.exp(masked - row_top)
    row_total = jnp.sum(expo_vals, axis=-1, keepdims=True)
    soft_low = (expo_vals / row_total).astype(BF16)
    mixed = jnp.einsum("hqk,khd->qhd", soft_low, heads_qkv[:, 2], preferred_element_type=F32)
    return mixed.reshape(count, wide // 3).astype(BF16), (row_top, row_total)


def attend_back(joined, places, stats, d_mixed):
    count, wide = joined.shape
    row_top, row_total = stats
    heads_qkv = joined.reshape(count, 3, -1, HEAD_DIM)
    d_mixed = d_mixed.reshape(count, -1, HEAD_DIM)
    masked = masked_scores(heads_qkv, places)
    weights_soft = jnp.exp(masked - row_top) / row_total
    soft_low = weights_soft.astype(BF16)
    d_values = jnp.einsum("hqk,qhd->khd", soft_low, d_mixed, preferred_element_type=F32)
    d_soft = jnp.einsum("qhd,khd->hqk", d_mixed, heads_qkv[:, 2], preferred_element_type=F32)
    d_scores = (
        weights_soft * (d_soft - jnp.sum(d_soft * weights_soft, axis=-1, keepdims=True))
    ).astype(BF16)
    scale = HEAD_DIM ** (-0.5)
    d_query = (
        jnp.einsum("hqk,khd->qhd", d_scores, heads_qkv[:, 1], preferred_element_type=F32) * scale
    )
    d_keys = (
        jnp.einsum("hqk,qhd->khd", d_scores, heads_qkv[:, 0], preferred_element_type=F32) * scale
    )
    return jnp.stack([d_query, d_keys, d_values], axis=1).reshape(count, wide).astype(BF16)


def gather_back(values, spread):
    high = lax.reduce_precision(values, 8, 7)
    low = (values - high).astype(BF16)
    return against(high.astype(BF16), spread) + against(low, spread)


def per_device(
    tokens, positions, cotangent, w_qkv, w_out, w_up, w_down, norm_gains, biases, up_bias
):
    data_devices = lax.axis_size("dp")
    links = Links(data_devices)
    core = links.core
    own = w_qkv.shape[1]
    pad = (own // 8 + 1) * 8
    feat = own * data_devices
    wide = pad * data_devices
    cols = w_up.shape[2]
    half = cols // 2
    count = tokens.shape[0] // 2
    down_half = w_down.shape[1] // 2

    def pick(if_first, if_second):
        return jnp.where(core == 0, if_first, if_second)

    orders = [links.order(core), links.order(1 - core)]

    def spread_of(order):
        column = jnp.arange(wide)
        place = column % pad
        target = jnp.where(place < own, jnp.repeat(order, pad) * own + place, -1)
        feature = lax.broadcasted_iota(jnp.int32, (feat, wide), 0)
        return (feature == target[None, :]).astype(BF16)

    spreads = [spread_of(order) for order in orders]
    spread_out = pick(spreads[1], spreads[0])
    order_small = pick(orders[0], orders[1])
    device = jnp.arange(data_devices)[:, None]
    to_device = (device == order_small[None, :]).astype(BF16)

    def halves_first(x):
        lead = x.shape[:-1]
        return x.reshape(lead + (data_devices, 2, down_half)).swapaxes(-3, -2).reshape(lead + (cols,))

    def halves_last(x):
        lead = x.shape[:-1]
        return x.reshape(lead + (2, data_devices, down_half)).swapaxes(-3, -2).reshape(lead + (cols,))

    small = jnp.concatenate([norm_gains[0].reshape(-1), biases[0].reshape(-1), up_bias[0]])
    small_size = small.shape[0]
    small = jnp.pad(small, (0, cols - small_size))[None]
    shard_qo = jnp.concatenate([w_qkv[0, :, : 2 * feat], w_out[0], w_qkv[0, :, 2 * feat :]], axis=1)
    shard_qo = jnp.concatenate([shard_qo, small, jnp.zeros((pad - own - 1, cols), BF16)], axis=0)
    shard_up = halves_first(jnp.pad(w_up[0], ((0, pad - own), (0, 0))))
    shard_down = w_down[0]

    def own_halves(shard, size, axis):
        keep = lax.dynamic_slice_in_dim(shard, core * size, size, axis)
        away = lax.dynamic_slice_in_dim(shard, (1 - core) * size, size, axis)
        other = links.swap_cores(away)
        return (pick(keep, other), pick(other, keep))

    halves_qo = own_halves(shard_qo, half, 1)
    halves_up = own_halves(shard_up, half, 1)
    halves_down = own_halves(shard_down, down_half, 0)
    gathers = []
    for layer in range(2):
        gathers.append(Gather(links, halves_qo[layer], False))
        gathers.append(Gather(links, halves_up[layer], False))
        gathers.append(Gather(links, halves_down[layer], True))

    source = lax.dynamic_slice_in_dim(tokens, core * count, count)
    places = lax.dynamic_slice_in_dim(positions, core * count, count)
    cotan = lax.dynamic_slice_in_dim(cotangent, core * count, count)
    states = [{}, {}]

    def forward_attention(layer, rows_in):
        s = states[layer]
        qo = gathers[3 * layer]
        weights = [qo.mine, qo.other]
        smalls = pick(qo.mine, qo.other).reshape(data_devices, pad, half)[:, own, :small_size]
        smalls = product(to_device, smalls)
        gains = smalls[:, : 2 * own].reshape(data_devices, 2, own)
        gains = gains.transpose(1, 0, 2).reshape(2, feat)
        shifts = smalls[:, 2 * own : 8 * own].reshape(data_devices, 6, own)
        shifts = shifts.transpose(1, 0, 2).reshape(6, feat)
        bias = halves_first(smalls[:, 8 * own :].reshape(-1))
        rows = rows_in.astype(F32)
        normed = norm_rows(rows, gains[0], shifts[0]).astype(BF16)
        normed = [product(normed, spread).astype(BF16) for spread in spreads]
        both = [product(normed[i], weights[i]) for i in range(2)]
        queries = pick(both[0], both[1])
        values = pick(both[1], both[0])[:, feat:]
        joined = jnp.concatenate(
            [queries[:, :feat] + shifts[1], queries[:, feat:], values + shifts[2]], axis=1
        ).astype(BF16)
        mixed, stats = attend(joined, places)
        mixed = product(mixed, spread_out).astype(BF16)
        w_out_all = pick(weights[1], weights[0])[:, :feat]
        hidden = rows + (product(mixed, w_out_all) + shifts[3])
        s.update(
            weights=weights, gains=gains, shifts=shifts, bias=bias, rows=rows, normed_one=normed,
            joined=joined, stats=stats, mixed=mixed, w_out=w_out_all, hidden=hidden,
        )
        return hidden

    def forward_up(layer):
        s = states[layer]
        up = gathers[3 * layer + 1]
        s["up"] = [up.mine, up.other]
        normed = norm_rows(s["hidden"], s["gains"][1], s["shifts"][4]).astype(BF16)
        s["normed_two"] = [product(normed, spread).astype(BF16) for spread in spreads]
        bias = s["bias"]
        bias = [pick(bias[:half], bias[half:]), pick(bias[half:], bias[:half])]
        s["inner"] = [product(s["normed_two"][i], s["up"][i]) + bias[i] for i in range(2)]
        s["active"] = [jax.nn.gelu(v, approximate=False).astype(BF16) for v in s["inner"]]
        return s["active"]

    def forward_down(layer):
        s = states[layer]
        down = gathers[3 * layer + 2]
        s["down"] = [down.mine, down.other]
        total = sum(product(s["active"][i], s["down"][i]) for i in range(2))
        return (s["hidden"] + (total + s["shifts"][5])).astype(BF16)

    def advance(jobs, slot, stages):
        for back, stage in enumerate(stages):
            if 0 <= slot - back < len(jobs):
                getattr(jobs[slot - back], stage)()

    going = ("stage_turn", "stage_second", "stage_first", "stage_swap")
    for slot in range(4):
        advance(gathers, slot, going)
        fence(gathers, ())
    advance(gathers, 4, going)
    fence(gathers, forward_attention(0, source))
    advance(gathers, 5, going)
    fence(gathers, forward_up(0))
    advance(gathers, 6, going)
    first_out = forward_down(0)
    fence(gathers, first_out)
    advance(gathers, 7, going)
    fence(gathers, forward_attention(1, first_out))
    advance(gathers, 8, going)
    forward_up(1)
    second_out = forward_down(1)

    def backward_down(layer, grad_rows):
        s = states[layer]
        grads = [outer_sum(s["active"][i], grad_rows).astype(BF16) for i in range(2)]
        s["grad_bdown"] = jnp.sum(grad_rows, axis=0, dtype=F32)
        s["d_inner"] = []
        for i in range(2):
            d_active = against(grad_rows, s["down"][i])
            back = jax.vjp(lambda v: jax.nn.gelu(v, approximate=False), s["inner"][i])[1]
            s["d_inner"].append(back(d_active)[0].astype(BF16))
        return Reduce(links, grads[0], grads[1], True), s["d_inner"]

    def backward_up(layer, grad_rows):
        s = states[layer]
        d_inner = s["d_inner"]
        grads = [outer_sum(s["normed_two"][i], d_inner[i]).astype(BF16) for i in range(2)]
        bups = [jnp.sum(d, axis=0, dtype=F32) for d in d_inner]
        s["grad_bup"] = halves_last(
            jnp.concatenate([pick(bups[0], bups[1]), pick(bups[1], bups[0])])
        )
        d_second = sum(gather_back(against(d_inner[i], s["up"][i]), spreads[i]) for i in range(2))
        back = jax.vjp(norm_rows, s["hidden"], s["gains"][1], s["shifts"][4])[1]
        d_hidden, s["grad_gain_two"], s["grad_shift_two"] = back(d_second)
        d_hidden = grad_rows.astype(F32) + d_hidden
        return Reduce(links, grads[0], grads[1], False), d_hidden

    def backward_attention(layer, d_hidden):
        s = states[layer]
        out_in = d_hidden.astype(BF16)
        grad_bout = jnp.sum(out_in, axis=0, dtype=F32)
        d_mixed = against(out_in, s["w_out"]).astype(BF16)
        d_mixed = against(d_mixed, spread_out).astype(BF16)
        d_joined = attend_back(s["joined"], places, s["stats"], d_mixed)
        sums = jnp.sum(d_joined, axis=0, dtype=F32)
        d_query, d_key, d_value = (d_joined[:, i * feat : (i + 1) * feat] for i in range(3))
        lone = jnp.zeros_like(d_value)
        kept = jnp.concatenate([d_query, d_key], axis=1)
        rest = jnp.concatenate([lone, d_value], axis=1)
        weights = s["weights"]
        d_first = gather_back(against(pick(kept, rest), weights[0]), spreads[0])
        d_first = d_first + gather_back(against(pick(rest, kept), weights[1]), spreads[1])
        back = jax.vjp(norm_rows, s["rows"], s["gains"][0], s["shifts"][0])[1]
        d_input, grad_gain_one, grad_shift_one = back(d_first)
        d_input = d_hidden + d_input
        small = [
            grad_gain_one, s["grad_gain_two"], grad_shift_one, sums[:feat], sums[2 * feat :],
            grad_bout, s["grad_shift_two"], s["grad_bdown"], s["grad_bup"],
        ]
        small = jnp.concatenate([v.reshape(data_devices, -1) for v in small], axis=1)
        small = outer_sum(to_device, small.astype(BF16)).astype(BF16)
        small = jnp.pad(small, ((0, 0), (0, half - small_size)))
        grads = []
        for i in range(2):
            has_query = core == i
            normed = s["normed_one"][i]
            left = jnp.concatenate([jnp.where(has_query, normed, s["mixed"]), normed], axis=0)
            one = jnp.where(has_query, d_query, out_in)
            two = jnp.where(has_query, d_key, d_value)
            right = jnp.concatenate(
                [jnp.concatenate([one, lone], axis=1), jnp.concatenate([lone, two], axis=1)], axis=0
            )
            grad = outer_sum(left, right).astype(BF16).reshape(data_devices, pad, half)
            row = lax.broadcasted_iota(jnp.int32, grad.shape, 1)
            grad = jnp.where((row == own) & has_query, small[:, None, :], grad)
            grads.append(grad.reshape(wide, half))
        return Reduce(links, grads[0], grads[1], False), d_input

    reduces = []
    returning = ("", "stage_swap", "stage_first", "stage_second", "stage_turn")

    def turn_back(slot, result):
        job, out = result
        reduces.append(job)
        for back in range(1, 5):
            if 0 <= slot - back < len(reduces):
                getattr(reduces[slot - back], returning[back])()
        return fence(reduces, out)

    slot = 0
    grad_in = cotan
    d_inputs = []
    for layer in (1, 0):
        states[layer]["d_inner"] = turn_back(slot, backward_down(layer, grad_in))
        d_hidden = turn_back(slot + 1, backward_up(layer, grad_in))
        d_input = turn_back(slot + 2, backward_attention(layer, d_hidden))
        d_inputs.append(d_input)
        grad_in = d_input.astype(BF16)
        slot += 3
    second_grad, first_grad = d_inputs
    for slot in range(6, 10):
        for back in range(1, 5):
            if 0 <= slot - back < len(reduces):
                getattr(reduces[slot - back], returning[back])()
        fence(reduces, ())
    down_second, up_second, qo_second, down_first, up_first, qo_first = [r.live[0] for r in reduces]

    def by_layer(first, second):
        mine = pick(first, second)
        other = links.swap_cores(pick(second, first))
        return pick(mine, other), pick(other, mine)

    acts = jnp.concatenate(by_layer(first_out, second_out), axis=0)[None]
    grads = jnp.concatenate(by_layer(first_grad, second_grad), axis=0)[None]
    query_key, out_value = [v.reshape(pad, half) for v in by_layer(qo_first, qo_second)]
    up = jnp.concatenate([v.reshape(pad, half) for v in by_layer(up_first, up_second)], axis=1)
    down = by_layer(down_first, down_second)
    down = jnp.concatenate([v.reshape(down_half, feat) for v in down], axis=0)
    smalls = query_key[own, :small_size]
    return (
        acts,
        grads,
        jnp.concatenate([query_key[:own], out_value[:own, feat:]], axis=1)[None],
        out_value[None, :own, :feat],
        halves_last(up[:own])[None],
        down[None],
        smalls[: 2 * own].reshape(1, 2, own),
        smalls[2 * own : 8 * own].reshape(1, 6, own),
        smalls[8 * own :][None],
    )


def solution(mesh):
    rows = P("dp", None)
    weight = P("section", "dp", None)
    vector = P("section", None, "dp")
    in_specs = (rows, P("dp"), rows, weight, weight, weight, weight, vector, vector, P("section", "dp"))
    out_specs = (weight, weight, weight, weight, weight, weight, vector, vector, P("section", "dp"))
    return jax.shard_map(
        per_device, mesh=mesh, in_specs=in_specs, out_specs=out_specs, check_vma=False
    )
```

time: 1430 us -> 1230 us (0.86)
  local copies, waits for them, and re-layouts: 249 us -> 133 us
  waiting for transfers between devices: 460 us -> 355 us
  starting transfers between devices: 161 us -> 76.5 us
  matrix products: 385 us -> 456 us
  other arithmetic: 168 us -> 194 us
    ppermute x80, waiting for transfers between devices: 460 us -> 355 us  [send(): return lax.ppermute(x, BOTH, perm)]
    ppermute x80, starting transfers between devices: 161 us -> 76.5 us  [send(): return lax.ppermute(x, BOTH, perm)]
    dynamic_update_slice x35 -> x8, local copies, waits for them, and re-layouts: 82.1 us -> 14.4 us  [stage_first(): lax.dynamic_update_slice_in_dim(out, part[:, None], links.quad ^ flip, 1)]
    concatenate x6 -> x3, local copies, waits for them, and re-layouts: 29.3 us -> 1.47 us  [the longest x1 1.26 us: per_device(): jnp.concatenate([w_qkv[0, :, :2 * feat], w_out[0], w_qkv[0, :, 2 * feat:]...]
    dot_general x16 -> x30, matrix products: 105 us -> 131 us  [against(): lax.dot_general(left, right, (((1,), (1,)), ((), ())), preferred_element_...]
    another operation x25 -> x11, local copies, waits for them, and re-layouts: 39.5 us -> 14.4 us
    dot_general x14 -> x26, matrix products: 123 us -> 147 us  [product(): return jnp.dot(left, right, preferred_element_type=F32)]
    reshape x18 -> x21, local copies, waits for them, and re-layouts: 4.64 us -> 28.4 us  [the longest x2 16.6 us: stage_swap(): mine = mine.reshape(-1, self.shape[1])]
  transfers between devices with their start and end apart: 80 -> 80, of which waited for: 27 -> 40; matrix products, arithmetic and copies ran while one was open for 33% -> 48% of each run, Pallas kernels for 0% -> 0%
where the time goes in v2:
time: 1230 us; the launch traced here: 1220 us
  matrix products  456 us (37%)
  waiting for transfers between devices  355 us (29%)
  other arithmetic  194 us (16%)
  local copies, waits for them, and re-layouts  133 us (11%)
  starting transfers between devices  76.5 us (6%)
    ppermute x80, waiting for transfers between devices, send(): return lax.ppermute(x, BOTH, perm)  355 us
    dot_general x26, matrix products, product(): return jnp.dot(left, right, preferred_element_type=F32)  147 us
    dot_general x30, matrix products, against(): lax.dot_general(left, right, (((1,), (1,)), ((), ())), preferred_element_...  131 us
    dot_general x14, matrix products, outer_sum(): lax.dot_general(left, right, (((0,), (0,)), ((), ())), preferred_element_...  84.2 us
    ppermute x80, starting transfers between devices, send(): return lax.ppermute(x, BOTH, perm)  76.5 us
    convert_element_type x4, local copies, waits for them, and re-layouts, backward_down(): outer_sum(s['active'][i], grad_rows).astype(BF16)  33.8 us
    convert_element_type x6, other arithmetic, stage_swap(): (keep.astype(F32) + self.links.swap_cores(away).astype(F32)).astype(BF16)  33.1 us
    convert_element_type x2, other arithmetic, attend_back(): d_scores = (weights_soft * (d_soft - jnp.sum(d_soft * weights_soft, axis=...  25.1 us
  transfers between devices with their start and end apart: 80, of which 40 were waited for; matrix products, arithmetic and copies ran while one was open for 48% of the time, Pallas kernels for 0%

profile of v2, /device:TPU:0, one launch (start us, length us, event | category | flops | bytes accessed | tf_op | source)
XLA Modules:
  0.0 1218.3 jit_solution(6237163662961966352)
XLA Ops:
  30.0 19.5 %collective-permute-done.2 = bf16[72,2176]{1,0:T(8,128)(2,1)S(1)} collective-permute-done((bf16[72,2176]{1,0:T(8,128)(2,1)S(1)}, bf16[72,2176]{1,0:T(8,128)(2,1)S(1)}, u32[]{:S(2)}, u32[]{:S(2)}) %collective-permute-start.2) | collective-permute-done | bytes 313376 | tf_op jit(solution)/shard_map/ppermute | solution.py:62
  60.9 20.3 %collective-permute-done.8 = bf16[72,2176]{1,0:T(8,128)(2,1)} collective-permute-done((bf16[72,2176]{1,0:T(8,128)(2,1)}, bf16[72,2176]{1,0:T(8,128)(2,1)}, u32[]{:S(2)}, u32[]{:S(2)}) %collective-permute-start.8) | collective-permute-done | bytes 313376 | tf_op jit(solution)/shard_map/ppermute | solution.py:62
  88.8 13.2 %collective-permute-done.12 = bf16[136,1088]{1,0:T(8,128)(2,1)S(1)} collective-permute-done((bf16[136,1088]{1,0:T(8,128)(2,1)S(1)}, bf16[136,1088]{1,0:T(8,128)(2,1)S(1)}, u32[]{:S(2)}, u32[]{:S(2)}) %collective-permute-start.12) | collective-permute-done | bytes 295968 | tf_op jit(solution)/shard_map/ppermute | solution.py:62
  117.6 10.9 collective-permute-done.10
  146.7 18.8 %collective-permute-done.19 = bf16[72,2176]{1,0:T(8,128)(2,1)} collective-permute-done((bf16[72,2176]{1,0:T(8,128)(2,1)S(1)}, bf16[72,2176]{1,0:T(8,128)(2,1)}, u32[]{:S(2)}, u32[]{:S(2)}) %collective-permute-start.19) | collective-permute-done | bytes 313376 | tf_op jit(solution)/shard_map/ppermute | solution.py:62
  193.4 16.7 %collective-permute-done.24 = bf16[72,2176]{1,0:T(8,128)(2,1)S(1)} collective-permute-done((bf16[72,2176]{1,0:T(8,128)(2,1)S(1)}, bf16[72,2176]{1,0:T(8,128)(2,1)S(1)}, u32[]{:S(2)}, u32[]{:S(2)}) %collective-permute-start.24) | collective-permute-done | bytes 313376 | tf_op jit(solution)/shard_map/ppermute | solution.py:62
  244.2 10.4 fusion.374
  280.4 16.6 %multiply_convert_fusion.5 = (bf16[512,2176]{1,0:T(8,128)(2,1)}, f32[512,2176]{1,0:T(8,128)}, f32[512,2176]{1,0:T(8,128)}) fusion(f32[2176]{0:T(1024)S(1)} %select_n.581, bf16[512,1152]{1,0:T(8,128)(2,1)S(1)} %fusion.137, bf16[1152,2176]{1,0:T(8,128)(2,1)} %bitcast.42), kind=kOutput, calls=%fused_computation.170 | convolution fusion | flops 2640445440 | bytes 17342976 | tf_op jit(solution)/shard_map/dot_general | solution.py:28
  316.1 23.2 %collective-permute-done.28 = bf16[2,4,72,2176]{3,2,1,0:T(8,128)(2,1)S(1)} collective-permute-done((bf16[2,4,72,2176]{3,2,1,0:T(8,128)(2,1)S(1)}, bf16[2,4,72,2176]{3,2,1,0:T(8,128)(2,1)S(1)}, u32[]{:S(2)}, u32[]{:S(2)}) %collective-permute-start.28) | collective-permute-done | bytes 2506784 | tf_op jit(solution)/shard_map/ppermute | solution.py:62
  342.1 16.4 %multiply_convert_fusion.4 = (bf16[512,2176]{1,0:T(8,128)(2,1)}, f32[512,2176]{1,0:T(8,128)}, f32[512,2176]{1,0:T(8,128)}) fusion(f32[2176]{0:T(1024)S(1)} %select_n.587, bf16[512,1152]{1,0:T(8,128)(2,1)S(1)} %fusion.133, bf16[1152,2176]{1,0:T(8,128)(2,1)} %collective-permute-done.26), kind=kOutput, calls=%fused_computation.157 | convolution fusion | flops 2640445440 | bytes 17342976 | tf_op jit(solution)/shard_map/dot_general | solution.py:28
  365.1 24.7 %collective-permute-done.35 = bf16[4,136,1088]{2,1,0:T(8,128)(2,1)} collective-permute-done((bf16[4,136,1088]{2,1,0:T(8,128)(2,1)}, bf16[4,136,1088]{2,1,0:T(8,128)(2,1)}, u32[]{:S(2)}, u32[]{:S(2)}) %collective-permute-start.35) | collective-permute-done | bytes 1183776 | tf_op jit(solution)/shard_map/ppermute | solution.py:62
  417.0 20.4 %collective-permute-done.36 = bf16[2,4,136,1088]{3,2,1,0:T(8,128)(2,1)} collective-permute-done((bf16[2,4,136,1088]{3,2,1,0:T(8,128)(2,1)}, bf16[2,4,136,1088]{3,2,1,0:T(8,128)(2,1)}, u32[]{:S(2)}, u32[]{:S(2)}) %collective-permute-start.36) | collective-permute-done | bytes 2367520 | tf_op jit(solution)/shard_map/ppermute | solution.py:62
  466.6 10.6 fusion.376
  505.4 16.7 %multiply_convert_fusion.3 = (bf16[512,2176]{1,0:T(8,128)(2,1)S(1)}, f32[512,2176]{1,0:T(8,128)}, f32[512,2176]{1,0:T(8,128)}) fusion(f32[2176]{0:T(1024)S(1)} %select_n.594, bf16[512,1152]{1,0:T(8,128)(2,1)} %fusion.139, bf16[1152,2176]{1,0:T(8,128)(2,1)} %bitcast.483), kind=kOutput, calls=%fused_computation.140 | convolution fusion | flops 2640445440 | bytes 17342976 | tf_op jit(solution)/shard_map/dot_general | solution.py:28
  547.3 16.0 %multiply_convert_fusion.2 = (bf16[512,2176]{1,0:T(8,128)(2,1)S(1)}, f32[512,2176]{1,0:T(8,128)}, f32[512,2176]{1,0:T(8,128)}) fusion(f32[2176]{0:T(1024)S(1)} %select_n.596, bf16[512,1152]{1,0:T(8,128)(2,1)S(1)} %fusion.135, bf16[1152,2176]{1,0:T(8,128)(2,1)} %collective-permute-done.37), kind=kOutput, calls=%fused_computation.127 | convolution fusion | flops 2640445440 | bytes 17342976 | tf_op jit(solution)/shard_map/dot_general | solution.py:28
  655.9 11.3 multiply_reduce_fusion.1
  667.2 12.6 %multiply_convert_fusion.1 = bf16[17,512,512]{1,2,0:T(8,128)(2,1)S(1)} fusion(f32[17,512,512]{1,2,0:T(8,128)} %get-tuple-element.405, f32[17,512]{1,0:T(8,128)S(1)} %get-tuple-element.404, f32[17,512,512]{1,2,0:T(8,128)} %get-tuple-element.396, f32[17,512]{1,0:T(8,128)S(1)} %copy-done.92), kind=kLoop, calls=%fused_computation.4 | loop fusion | flops 17825792 | bytes 44634112 | tf_op jit(solution)/shard_map/convert_element_type | solution.py:220
  863.5 12.8 %collective-permute-done.47 = bf16[136,1088]{1,0:T(8,128)(2,1)S(1)} collective-permute-done((bf16[136,1088]{1,0:T(8,128)(2,1)}, bf16[136,1088]{1,0:T(8,128)(2,1)S(1)}, u32[]{:S(2)}, u32[]{:S(2)}) %collective-permute-start.47) | collective-permute-done | bytes 295968 | tf_op jit(solution)/shard_map/ppermute | solution.py:62
  899.2 10.4 fusion.249
  909.6 11.6 multiply_reduce_fusion
  921.2 12.6 %multiply_convert_fusion = bf16[17,512,512]{1,2,0:T(8,128)(2,1)S(1)} fusion(f32[17,512,512]{1,2,0:T(8,128)} %get-tuple-element.411, f32[17,512]{1,0:T(8,128)S(1)} %get-tuple-element.410, f32[17,512,512]{1,2,0:T(8,128)} %get-tuple-element.386, f32[17,512]{1,0:T(8,128)S(1)} %copy-done.90), kind=kLoop, calls=%fused_computation.2 | loop fusion | flops 17825792 | bytes 44634112 | tf_op jit(solution)/shard_map/convert_element_type | solution.py:220
  981.4 10.2 convolution_convert_fusion.5
  1009.2 10.5 collective-permute-done.55
  1067.4 12.5 %collective-permute-done.60 = bf16[72,2176]{1,0:T(8,128)(2,1)S(1)} collective-permute-done((bf16[72,2176]{1,0:T(8,128)(2,1)S(1)}, bf16[72,2176]{1,0:T(8,128)(2,1)S(1)}, u32[]{:S(2)}, u32[]{:S(2)}) %collective-permute-start.60) | collective-permute-done | bytes 313376 | tf_op jit(solution)/shard_map/ppermute | solution.py:62
  (837 shorter events, 855.5 us)
Async XLA Ops:
  131.2 44.0 %collective-permute-start.16 = (bf16[2,4,72,2176]{3,2,1,0:T(8,128)(2,1)S(1)}, bf16[2,4,72,2176]{3,2,1,0:T(8,128)(2,1)}, u32[]{:S(2)}, u32[]{:S(2)}) collective-permute-start(bf16[2,4,72,2176]{3,2,1,0:T(8,128)(2,1)S(1)} %pad_maximum_fusion.5), channel_id=1, source_target_pairs={{0,2},{1,3},{2,0},{3,1},{4,6},{5,7},{6,4},{7,5},{8,10},{9,11},{10,... | collective-permute-start | bytes 7520264 | tf_op jit(solution)/shard_map/ppermute | solution.py:62
  146.2 79.6 %collective-permute-start.15 = (bf16[1152,2176]{1,0:T(8,128)(2,1)}, bf16[1152,2176]{1,0:T(8,128)(2,1)}, u32[]{:S(2)}, u32[]{:S(2)}) collective-permute-start(bf16[1152,2176]{1,0:T(8,128)(2,1)} %bitcast.438), channel_id=1, source_target_pairs={{0,16},{1,17},{2,18},{3,19},{4,20},{5,21},{6,22},{7,23},{8,24},{9,... | collective-permute-start | bytes 15040520 | tf_op jit(solution)/shard_map/ppermute | solution.py:62
  179.7 43.9 %collective-permute-start.21 = (bf16[2,4,136,1088]{3,2,1,0:T(8,128)(2,1)S(1)}, bf16[2,4,136,1088]{3,2,1,0:T(8,128)(2,1)S(1)}, u32[]{:S(2)}, u32[]{:S(2)}) collective-permute-start(bf16[2,4,136,1088]{3,2,1,0:T(8,128)(2,1)S(1)} %pad_maximum_fusion.6), channel_id=1, source_target_pairs={{0,2},{1,3},{2,0},{3,1},{4,6},{5,7},{6,4},{7,5},{8,10},{9,11},{10,... | collective-permute-start | bytes 7102472 | tf_op jit(solution)/shard_map/ppermute | solution.py:62
  210.1 132.0 %collective-permute-start.26 = (bf16[1152,2176]{1,0:T(8,128)(2,1)}, bf16[1152,2176]{1,0:T(8,128)(2,1)}, u32[]{:S(2)}, u32[]{:S(2)}) collective-permute-start(bf16[1152,2176]{1,0:T(8,128)(2,1)} %bitcast.42), channel_id=1, source_target_pairs={{0,16},{1,17},{2,18},{3,19},{4,20},{5,21},{6,22},{7,23},{8,24},{9,... | collective-permute-start | bytes 15040520 | tf_op jit(solution)/shard_map/ppermute | solution.py:62
  269.9 40.5 %collective-permute-start.32 = (bf16[136,1088]{1,0:T(8,128)(2,1)S(1)}, bf16[136,1088]{1,0:T(8,128)(2,1)S(1)}, u32[]{:S(2)}, u32[]{:S(2)}) collective-permute-start(bf16[136,1088]{1,0:T(8,128)(2,1)S(1)} %get-tuple-element.133), channel_id=1, source_target_pairs={{0,4},{1,5},{2,6},{3,7},{4,8},{5,9},{6,10},{7,11},{8,12},{9,13},{1... | collective-permute-start | bytes 887816 | tf_op jit(solution)/shard_map/ppermute | solution.py:62
  310.2 83.1 %collective-permute-start.27 = (bf16[2176,1088]{0,1:T(8,128)(2,1)}, bf16[2176,1088]{0,1:T(8,128)(2,1)}, u32[]{:S(2)}, u32[]{:S(2)}) collective-permute-start(bf16[2176,1088]{0,1:T(8,128)(2,1)} %copy.295), channel_id=1, source_target_pairs={{0,16},{1,17},{2,18},{3,19},{4,20},{5,21},{6,22},{7,23},{8,24},{9,... | collective-permute-start | bytes 14204936 | tf_op jit(solution)/shard_map/ppermute | solution.py:62
  358.5 42.9 %collective-permute-start.34 = (bf16[2,4,72,2176]{3,2,1,0:T(8,128)(2,1)}, bf16[2,4,72,2176]{3,2,1,0:T(8,128)(2,1)}, u32[]{:S(2)}, u32[]{:S(2)}) collective-permute-start(bf16[2,4,72,2176]{3,2,1,0:T(8,128)(2,1)} %pad_maximum_fusion.8), channel_id=1, source_target_pairs={{0,2},{1,3},{2,0},{3,1},{4,6},{5,7},{6,4},{7,5},{8,10},{9,11},{10,... | collective-permute-start | bytes 7520264 | tf_op jit(solution)/shard_map/ppermute | solution.py:62
  365.0 77.3 %collective-permute-start.33 = (bf16[1152,2176]{1,0:T(8,128)(2,1)}, bf16[1152,2176]{1,0:T(8,128)(2,1)}, u32[]{:S(2)}, u32[]{:S(2)}) collective-permute-start(bf16[1152,2176]{1,0:T(8,128)(2,1)} %bitcast.65), channel_id=1, source_target_pairs={{0,16},{1,17},{2,18},{3,19},{4,20},{5,21},{6,22},{7,23},{8,24},{9,... | collective-permute-start | bytes 15040520 | tf_op jit(solution)/shard_map/ppermute | solution.py:62
  409.5 137.8 %collective-permute-start.37 = (bf16[1152,2176]{1,0:T(8,128)(2,1)}, bf16[1152,2176]{1,0:T(8,128)(2,1)}, u32[]{:S(2)}, u32[]{:S(2)}) collective-permute-start(bf16[1152,2176]{1,0:T(8,128)(2,1)} %bitcast.482), channel_id=1, source_target_pairs={{0,16},{1,17},{2,18},{3,19},{4,20},{5,21},{6,22},{7,23},{8,24},{9,... | collective-permute-start | bytes 15040520 | tf_op jit(solution)/shard_map/ppermute | solution.py:62
  505.4 72.4 %collective-permute-start.38 = (bf16[2176,1088]{0,1:T(8,128)(2,1)}, bf16[2176,1088]{0,1:T(8,128)(2,1)}, u32[]{:S(2)}, u32[]{:S(2)}) collective-permute-start(bf16[2176,1088]{0,1:T(8,128)(2,1)} %copy.305), channel_id=1, source_target_pairs={{0,16},{1,17},{2,18},{3,19},{4,20},{5,21},{6,22},{7,23},{8,24},{9,... | collective-permute-start | bytes 14204936 | tf_op jit(solution)/shard_map/ppermute | solution.py:62
  690.0 56.8 %collective-permute-start.41 = (bf16[2,4,136,1088]{3,2,1,0:T(8,128)(2,1)}, bf16[2,4,136,1088]{3,2,1,0:T(8,128)(2,1)}, u32[]{:S(2)}, u32[]{:S(2)}) collective-permute-start(bf16[2,4,136,1088]{3,2,1,0:T(8,128)(2,1)} %pad_maximum_fusion.10), channel_id=1, source_target_pairs={{0,2},{1,3},{2,0},{3,1},{4,6},{5,7},{6,4},{7,5},{8,10},{9,11},{10,... | collective-permute-start | bytes 7102472 | tf_op jit(solution)/shard_map/ppermute | solution.py:62
  690.8 60.1 %collective-permute-start.42 = (bf16[16,72,2176]{2,1,0:T(8,128)(2,1)}, bf16[16,72,2176]{2,1,0:T(8,128)(2,1)}, u32[]{:S(2)}, u32[]{:S(2)}) collective-permute-start(bf16[16,72,2176]{2,1,0:T(8,128)(2,1)} %bitcast.530), channel_id=1, source_target_pairs={{0,16},{1,17},{2,18},{3,19},{4,20},{5,21},{6,22},{7,23},{8,24},{9,... | collective-permute-start | bytes 15040520 | tf_op jit(solution)/shard_map/ppermute | solution.py:62
  756.2 55.7 %collective-permute-start.45 = (bf16[16,72,2176]{2,1,0:T(8,128)(2,1)}, bf16[16,72,2176]{2,1,0:T(8,128)(2,1)}, u32[]{:S(2)}, u32[]{:S(2)}) collective-permute-start(bf16[16,72,2176]{2,1,0:T(8,128)(2,1)} %get-tuple-element.152), channel_id=1, source_target_pairs={{0,16},{1,17},{2,18},{3,19},{4,20},{5,21},{6,22},{7,23},{8,24},{9,... | collective-permute-start | bytes 15040520 | tf_op jit(solution)/shard_map/ppermute | solution.py:62
  759.0 47.9 %collective-permute-start.44 = (bf16[2,4,72,2176]{3,2,1,0:T(8,128)(2,1)}, bf16[2,4,72,2176]{3,2,1,0:T(8,128)(2,1)}, u32[]{:S(2)}, u32[]{:S(2)}) collective-permute-start(bf16[2,4,72,2176]{3,2,1,0:T(8,128)(2,1)} %bitcast.110), channel_id=1, source_target_pairs={{0,2},{1,3},{2,0},{3,1},{4,6},{5,7},{6,4},{7,5},{8,10},{9,11},{10,... | collective-permute-start | bytes 7520264 | tf_op jit(solution)/shard_map/ppermute | solution.py:62
  824.8 53.6 %collective-permute-start.49 = (bf16[4,72,2176]{2,1,0:T(8,128)(2,1)}, bf16[4,72,2176]{2,1,0:T(8,128)(2,1)}, u32[]{:S(2)}, u32[]{:S(2)}) collective-permute-start(bf16[4,72,2176]{2,1,0:T(8,128)(2,1)} %get-tuple-element.156), channel_id=1, source_target_pairs={{0,1},{1,0},{2,3},{3,2},{4,5},{5,4},{6,7},{7,6},{8,9},{9,8},{10,11... | collective-permute-start | bytes 3760136 | tf_op jit(solution)/shard_map/ppermute | solution.py:62
  842.7 42.1 %collective-permute-start.51 = (bf16[16,136,1088]{2,1,0:T(8,128)(2,1)}, bf16[16,136,1088]{2,1,0:T(8,128)(2,1)}, u32[]{:S(2)}, u32[]{:S(2)}) collective-permute-start(bf16[16,136,1088]{2,1,0:T(8,128)(2,1)} %bitcast.114), channel_id=1, source_target_pairs={{0,16},{1,17},{2,18},{3,19},{4,20},{5,21},{6,22},{7,23},{8,24},{9,... | collective-permute-start | bytes 14204936 | tf_op jit(solution)/shard_map/ppermute | solution.py:62
  941.2 61.2 %collective-permute-start.52 = (bf16[72,2176]{1,0:T(8,128)(2,1)}, bf16[72,2176]{1,0:T(8,128)(2,1)S(1)}, u32[]{:S(2)}, u32[]{:S(2)}) collective-permute-start(bf16[72,2176]{1,0:T(8,128)(2,1)} %get-tuple-element.350), channel_id=1, source_target_pairs={{0,12},{1,13},{2,14},{3,15},{4,0},{5,1},{6,2},{7,3},{8,4},{9,5},{1... | collective-permute-start | bytes 940040 | tf_op jit(solution)/shard_map/ppermute | solution.py:62
  941.7 65.2 %collective-permute-start.54 = (bf16[72,2176]{1,0:T(8,128)(2,1)}, bf16[72,2176]{1,0:T(8,128)(2,1)}, u32[]{:S(2)}, u32[]{:S(2)}) collective-permute-start(bf16[72,2176]{1,0:T(8,128)(2,1)} %get-tuple-element.351), channel_id=1, source_target_pairs={{0,4},{1,5},{2,6},{3,7},{4,8},{5,9},{6,10},{7,11},{8,12},{9,13},{1... | collective-permute-start | bytes 940040 | tf_op jit(solution)/shard_map/ppermute | solution.py:62
  943.2 63.7 %collective-permute-start.53 = (bf16[72,2176]{1,0:T(8,128)(2,1)}, bf16[72,2176]{1,0:T(8,128)(2,1)}, u32[]{:S(2)}, u32[]{:S(2)}) collective-permute-start(bf16[72,2176]{1,0:T(8,128)(2,1)} %get-tuple-element.352), channel_id=1, source_target_pairs={{0,8},{1,9},{2,10},{3,11},{4,12},{5,13},{6,14},{7,15},{8,0},{9,1},... | collective-permute-start | bytes 940040 | tf_op jit(solution)/shard_map/ppermute | solution.py:62
  947.0 74.1 %collective-permute-start.56 = (bf16[2,4,136,1088]{3,2,1,0:T(8,128)(2,1)}, bf16[2,4,136,1088]{3,2,1,0:T(8,128)(2,1)}, u32[]{:S(2)}, u32[]{:S(2)}) collective-permute-start(bf16[2,4,136,1088]{3,2,1,0:T(8,128)(2,1)} %pad_maximum_fusion.11), channel_id=1, source_target_pairs={{0,2},{1,3},{2,0},{3,1},{4,6},{5,7},{6,4},{7,5},{8,10},{9,11},{10,... | collective-permute-start | bytes 7102472 | tf_op jit(solution)/shard_map/ppermute | solution.py:62
  948.2 76.7 %collective-permute-start.57 = (bf16[16,72,2176]{2,1,0:T(8,128)(2,1)}, bf16[16,72,2176]{2,1,0:T(8,128)(2,1)}, u32[]{:S(2)}, u32[]{:S(2)}) collective-permute-start(bf16[16,72,2176]{2,1,0:T(8,128)(2,1)} %bitcast.529), channel_id=1, source_target_pairs={{0,16},{1,17},{2,18},{3,19},{4,20},{5,21},{6,22},{7,23},{8,24},{9,... | collective-permute-start | bytes 15040520 | tf_op jit(solution)/shard_map/ppermute | solution.py:62
  1032.4 59.1 %collective-permute-start.64 = (bf16[16,72,2176]{2,1,0:T(8,128)(2,1)}, bf16[16,72,2176]{2,1,0:T(8,128)(2,1)}, u32[]{:S(2)}, u32[]{:S(2)}) collective-permute-start(bf16[16,72,2176]{2,1,0:T(8,128)(2,1)} %get-tuple-element.178), channel_id=1, source_target_pairs={{0,16},{1,17},{2,18},{3,19},{4,20},{5,21},{6,22},{7,23},{8,24},{9,... | collective-permute-start | bytes 15040520 | tf_op jit(solution)/shard_map/ppermute | solution.py:62
  1046.9 43.9 %collective-permute-start.63 = (bf16[2,4,72,2176]{3,2,1,0:T(8,128)(2,1)S(1)}, bf16[2,4,72,2176]{3,2,1,0:T(8,128)(2,1)S(1)}, u32[]{:S(2)}, u32[]{:S(2)}) collective-permute-start(bf16[2,4,72,2176]{3,2,1,0:T(8,128)(2,1)S(1)} %bitcast.503), channel_id=1, source_target_pairs={{0,2},{1,3},{2,0},{3,1},{4,6},{5,7},{6,4},{7,5},{8,10},{9,11},{10,... | collective-permute-start | bytes 7520264 | tf_op jit(solution)/shard_map/ppermute | solution.py:62
  1095.5 43.9 %collective-permute-start.69 = (bf16[2,4,72,2176]{3,2,1,0:T(8,128)(2,1)S(1)}, bf16[2,4,72,2176]{3,2,1,0:T(8,128)(2,1)S(1)}, u32[]{:S(2)}, u32[]{:S(2)}) collective-permute-start(bf16[2,4,72,2176]{3,2,1,0:T(8,128)(2,1)S(1)} %bitcast.502), channel_id=1, source_target_pairs={{0,2},{1,3},{2,0},{3,1},{4,6},{5,7},{6,4},{7,5},{8,10},{9,11},{10,... | collective-permute-start | bytes 7520264 | tf_op jit(solution)/shard_map/ppermute | solution.py:62
  (222 other events, 3178.0 us)

commit v3 on v2

--- a/solution.py
+++ b/solution.py
@@ -119,8 +119,7 @@
     def stage_swap(self):
         (mine,) = self.live
         mine = mine.reshape(-1, self.shape[1])
-        self.mine, self.other = mine, self.links.swap_cores(mine)
-        self.live = []
+        self.live = [mine, self.links.swap_cores(mine)]
 
 
 class Reduce:
@@ -306,8 +305,8 @@
     def forward_attention(layer, rows_in):
         s = states[layer]
         qo = gathers[3 * layer]
-        weights = [qo.mine, qo.other]
-        smalls = pick(qo.mine, qo.other).reshape(data_devices, pad, half)[:, own, :small_size]
+        weights = list(qo.live)
+        smalls = pick(weights[0], weights[1]).reshape(data_devices, pad, half)[:, own, :small_size]
         smalls = product(to_device, smalls)
         gains = smalls[:, : 2 * own].reshape(data_devices, 2, own)
         gains = gains.transpose(1, 0, 2).reshape(2, feat)
@@ -336,7 +335,7 @@
     def forward_up(layer):
         s = states[layer]
         up = gathers[3 * layer + 1]
-        s["up"] = [up.mine, up.other]
+        s["up"] = list(up.live)
         normed = norm_rows(s["hidden"], s["gains"][1], s["shifts"][4]).astype(BF16)
         s["normed_two"] = [product(normed, spread).astype(BF16) for spread in spreads]
         bias = s["bias"]
@@ -348,7 +347,7 @@
     def forward_down(layer):
         s = states[layer]
         down = gathers[3 * layer + 2]
-        s["down"] = [down.mine, down.other]
+        s["down"] = list(down.live)
         total = sum(product(s["active"][i], s["down"][i]) for i in range(2))
         return (s["hidden"] + (total + s["shifts"][5])).astype(BF16)
 
@@ -358,20 +357,20 @@
                 getattr(jobs[slot - back], stage)()
 
     going = ("stage_turn", "stage_second", "stage_first", "stage_swap")
+    def forward_slot(slot, compute, *args):
+        advance(gathers, slot, going)
+        out = compute(*args) if compute else ()
+        if slot >= 8:
+            return out
+        return fence(gathers, out)
+
     for slot in range(4):
-        advance(gathers, slot, going)
-        fence(gathers, ())
-    advance(gathers, 4, going)
-    fence(gathers, forward_attention(0, source))
-    advance(gathers, 5, going)
-    fence(gathers, forward_up(0))
-    advance(gathers, 6, going)
-    first_out = forward_down(0)
-    fence(gathers, first_out)
-    advance(gathers, 7, going)
-    fence(gathers, forward_attention(1, first_out))
-    advance(gathers, 8, going)
-    forward_up(1)
+        forward_slot(slot, None)
+    states[0]["hidden"] = forward_slot(4, forward_attention, 0, source)
+    states[0]["active"] = forward_slot(5, forward_up, 0)
+    first_out = forward_slot(6, forward_down, 0)
+    states[1]["hidden"] = forward_slot(7, forward_attention, 1, first_out)
+    states[1]["active"] = forward_slot(8, forward_up, 1)
     second_out = forward_down(1)
 
     def backward_down(layer, grad_rows):
@@ -402,10 +401,14 @@
     def backward_attention(layer, d_hidden):
         s = states[layer]
         out_in = d_hidden.astype(BF16)
-        grad_bout = jnp.sum(out_in, axis=0, dtype=F32)
         d_mixed = against(out_in, s["w_out"]).astype(BF16)
         d_mixed = against(d_mixed, spread_out).astype(BF16)
-        d_joined = attend_back(s["joined"], places, s["stats"], d_mixed)
+        return attend_back(s["joined"], places, s["stats"], d_mixed)
+
+    def backward_input(layer, d_hidden, d_joined):
+        s = states[layer]
+        out_in = d_hidden.astype(BF16)
+        grad_bout = jnp.sum(out_in, axis=0, dtype=F32)
         sums = jnp.sum(d_joined, axis=0, dtype=F32)
         d_query, d_key, d_value = (d_joined[:, i * feat : (i + 1) * feat] for i in range(3))
         lone = jnp.zeros_like(d_value)
@@ -443,12 +446,24 @@
     reduces = []
     returning = ("", "stage_swap", "stage_first", "stage_second", "stage_turn")
 
+    def by_layer(first, second):
+        mine = pick(first, second)
+        other = links.swap_cores(pick(second, first))
+        return pick(mine, other), pick(other, mine)
+
+    begun = []
+
+    def advance_back(slot):
+        for job, start in zip(reduces, begun):
+            if 1 <= slot - start < 5:
+                getattr(job, returning[slot - start])()
+
     def turn_back(slot, result):
         job, out = result
-        reduces.append(job)
-        for back in range(1, 5):
-            if 0 <= slot - back < len(reduces):
-                getattr(reduces[slot - back], returning[back])()
+        if job is not None:
+            reduces.append(job)
+            begun.append(slot)
+        advance_back(slot)
         return fence(reduces, out)
 
     slot = 0
@@ -457,28 +472,31 @@
     for layer in (1, 0):
         states[layer]["d_inner"] = turn_back(slot, backward_down(layer, grad_in))
         d_hidden = turn_back(slot + 1, backward_up(layer, grad_in))
-        d_input = turn_back(slot + 2, backward_attention(layer, d_hidden))
+        d_hidden, d_joined = turn_back(
+            slot + 2, (None, (d_hidden, backward_attention(layer, d_hidden)))
+        )
+        d_input = turn_back(slot + 3, backward_input(layer, d_hidden, d_joined))
         d_inputs.append(d_input)
         grad_in = d_input.astype(BF16)
-        slot += 3
+        slot += 4
     second_grad, first_grad = d_inputs
-    for slot in range(6, 10):
-        for back in range(1, 5):
-            if 0 <= slot - back < len(reduces):
-                getattr(reduces[slot - back], returning[back])()
-        fence(reduces, ())
-    down_second, up_second, qo_second, down_first, up_first, qo_first = [r.live[0] for r in reduces]
-
-    def by_layer(first, second):
-        mine = pick(first, second)
-        other = links.swap_cores(pick(second, first))
-        return pick(mine, other), pick(other, mine)
+    for slot in range(8, 12):
+        advance_back(slot)
+        if slot == 11:
+            down_second, up_second, qo_second, down_first, up_first, qo_first = [
+                r.live[0] for r in reduces
+            ]
+            up, down = fence(
+                reduces, (by_layer(up_first, up_second), by_layer(down_first, down_second))
+            )
+            qo_first = reduces[-1].live[0]
+        else:
+            fence(reduces, ())
 
     acts = jnp.concatenate(by_layer(first_out, second_out), axis=0)[None]
     grads = jnp.concatenate(by_layer(first_grad, second_grad), axis=0)[None]
     query_key, out_value = [v.reshape(pad, half) for v in by_layer(qo_first, qo_second)]
-    up = jnp.concatenate([v.reshape(pad, half) for v in by_layer(up_first, up_second)], axis=1)
-    down = by_layer(down_first, down_second)
+    up = jnp.concatenate([v.reshape(pad, half) for v in up], axis=1)
     down = jnp.concatenate([v.reshape(down_half, feat) for v in down], axis=0)
     smalls = query_key[own, :small_size]
     return (

time: 1230 us -> 1220 us (level)
  waiting for transfers between devices: 355 us -> 274 us
  local copies, waits for them, and re-layouts: 133 us -> 152 us
  starting transfers between devices: 76.5 us -> 94.5 us
  other arithmetic: 194 us -> 211 us
    ppermute x80, waiting for transfers between devices: 355 us -> 274 us  [send(): return lax.ppermute(x, BOTH, perm)]
    ppermute x80, starting transfers between devices: 76.5 us -> 94.5 us  [send(): return lax.ppermute(x, BOTH, perm)]
  transfers between devices with their start and end apart: 80 -> 80, of which waited for: 40 -> 28; matrix products, arithmetic and copies ran while one was open for 48% -> 51% of each run, Pallas kernels for 0% -> 0%
where the time goes in v3:
time: 1220 us; the launch traced here: 1200 us
  matrix products  468 us (38%)
  waiting for transfers between devices  274 us (22%)
  other arithmetic  211 us (17%)
  local copies, waits for them, and re-layouts  152 us (12%)
  starting transfers between devices  94.5 us (8%)
    ppermute x80, waiting for transfers between devices, send(): return lax.ppermute(x, BOTH, perm)  274 us
    dot_general x26, matrix products, product(): return jnp.dot(left, right, preferred_element_type=F32)  151 us
    dot_general x30, matrix products, against(): lax.dot_general(left, right, (((1,), (1,)), ((), ())), preferred_element_...  137 us
    ppermute x80, starting transfers between devices, send(): return lax.ppermute(x, BOTH, perm)  94.5 us
    dot_general x14, matrix products, outer_sum(): lax.dot_general(left, right, (((0,), (0,)), ((), ())), preferred_element_...  88.8 us
    convert_element_type x6, other arithmetic, stage_swap(): (keep.astype(F32) + self.links.swap_cores(away).astype(F32)).astype(BF16)  35.3 us
    convert_element_type x4, local copies, waits for them, and re-layouts, backward_down(): outer_sum(s['active'][i], grad_rows).astype(BF16)  33.5 us
    convert_element_type x2, other arithmetic, attend_back(): d_scores = (weights_soft * (d_soft - jnp.sum(d_soft * weights_soft, axis=...  25.3 us
  transfers between devices with their start and end apart: 80, of which 28 were waited for; matrix products, arithmetic and copies ran while one was open for 51% of the time, Pallas kernels for 0%

profile of v3, /device:TPU:0, one launch (start us, length us, event | category | flops | bytes accessed | tf_op | source)
XLA Modules:
  0.0 1204.7 jit_solution(15058672544944739503)
XLA Ops:
  30.7 19.5 %collective-permute-done.2 = bf16[72,2176]{1,0:T(8,128)(2,1)S(1)} collective-permute-done((bf16[72,2176]{1,0:T(8,128)(2,1)S(1)}, bf16[72,2176]{1,0:T(8,128)(2,1)S(1)}, u32[]{:S(2)}, u32[]{:S(2)}) %collective-permute-start.2) | collective-permute-done | bytes 313376 | tf_op jit(solution)/shard_map/ppermute | solution.py:62
  61.7 20.3 %collective-permute-done.8 = bf16[72,2176]{1,0:T(8,128)(2,1)} collective-permute-done((bf16[72,2176]{1,0:T(8,128)(2,1)}, bf16[72,2176]{1,0:T(8,128)(2,1)}, u32[]{:S(2)}, u32[]{:S(2)}) %collective-permute-start.8) | collective-permute-done | bytes 313376 | tf_op jit(solution)/shard_map/ppermute | solution.py:62
  89.6 13.2 %collective-permute-done.12 = bf16[136,1088]{1,0:T(8,128)(2,1)S(1)} collective-permute-done((bf16[136,1088]{1,0:T(8,128)(2,1)S(1)}, bf16[136,1088]{1,0:T(8,128)(2,1)S(1)}, u32[]{:S(2)}, u32[]{:S(2)}) %collective-permute-start.12) | collective-permute-done | bytes 295968 | tf_op jit(solution)/shard_map/ppermute | solution.py:62
  118.3 10.9 collective-permute-done.10
  148.3 14.7 %collective-permute-start.18 = (bf16[72,2176]{1,0:T(8,128)(2,1)S(1)}, bf16[72,2176]{1,0:T(8,128)(2,1)S(1)}, u32[]{:S(2)}, u32[]{:S(2)}) collective-permute-start(bf16[72,2176]{1,0:T(8,128)(2,1)S(1)} %get-tuple-element.147), channel_id=1, source_target_pairs={{0,4},{1,5},{2,6},{3,7},{4,8},{5,9},{6,10},{7,11},{8,12},{9,13},{1... | collective-permute-start | bytes 940040 | tf_op jit(solution)/shard_map/ppermute | solution.py:62
  208.2 10.3 fusion.386
  287.2 16.7 %multiply_convert_fusion.5 = (bf16[512,2176]{1,0:T(8,128)(2,1)}, f32[512,2176]{1,0:T(8,128)}, f32[512,2176]{1,0:T(8,128)}) fusion(f32[2176]{0:T(1024)S(1)} %select_n.585, bf16[512,1152]{1,0:T(8,128)(2,1)} %fusion.137, bf16[1152,2176]{1,0:T(8,128)(2,1)} %bitcast.30), kind=kOutput, calls=%fused_computation.168 | convolution fusion | flops 2640445440 | bytes 17342976 | tf_op jit(solution)/shard_map/dot_general | solution.py:28
  303.9 16.4 %multiply_convert_fusion.4 = (bf16[512,2176]{1,0:T(8,128)(2,1)}, f32[512,2176]{1,0:T(8,128)}, f32[512,2176]{1,0:T(8,128)}) fusion(f32[2176]{0:T(1024)S(1)} %select_n.587, bf16[512,1152]{1,0:T(8,128)(2,1)S(1)} %copy-done.141, bf16[1152,2176]{1,0:T(8,128)(2,1)} %collective-permute-done.21), kind=kOutput, calls=%fused_computation.155 | convolution fusion | flops 2640445440 | bytes 17342976 | tf_op jit(solution)/shard_map/dot_general | solution.py:28
  332.3 18.4 %collective-permute-done.28 = bf16[2,4,72,2176]{3,2,1,0:T(8,128)(2,1)S(1)} collective-permute-done((bf16[2,4,72,2176]{3,2,1,0:T(8,128)(2,1)S(1)}, bf16[2,4,72,2176]{3,2,1,0:T(8,128)(2,1)S(1)}, u32[]{:S(2)}, u32[]{:S(2)}) %collective-permute-start.28) | collective-permute-done | bytes 2506784 | tf_op jit(solution)/shard_map/ppermute | solution.py:62
  369.7 18.2 %collective-permute-done.35 = bf16[4,136,1088]{2,1,0:T(8,128)(2,1)S(1)} collective-permute-done((bf16[4,136,1088]{2,1,0:T(8,128)(2,1)}, bf16[4,136,1088]{2,1,0:T(8,128)(2,1)S(1)}, u32[]{:S(2)}, u32[]{:S(2)}) %collective-permute-start.35) | collective-permute-done | bytes 1183776 | tf_op jit(solution)/shard_map/ppermute | solution.py:62
  428.9 10.7 fusion.387
  484.8 16.7 %multiply_convert_fusion.3 = (bf16[512,2176]{1,0:T(8,128)(2,1)S(1)}, f32[512,2176]{1,0:T(8,128)}, f32[512,2176]{1,0:T(8,128)}) fusion(f32[2176]{0:T(1024)S(1)} %select_n.594, bf16[512,1152]{1,0:T(8,128)(2,1)} %fusion.139, bf16[1152,2176]{1,0:T(8,128)(2,1)} %bitcast.68), kind=kOutput, calls=%fused_computation.138 | convolution fusion | flops 2640445440 | bytes 17342976 | tf_op jit(solution)/shard_map/dot_general | solution.py:28
  515.7 16.5 %multiply_convert_fusion.2 = (bf16[512,2176]{1,0:T(8,128)(2,1)S(1)}, f32[512,2176]{1,0:T(8,128)}, f32[512,2176]{1,0:T(8,128)}) fusion(f32[2176]{0:T(1024)S(1)} %select_n.596, bf16[512,1152]{1,0:T(8,128)(2,1)} %fusion.135, bf16[1152,2176]{1,0:T(8,128)(2,1)} %collective-permute-done.36), kind=kOutput, calls=%fused_computation.125 | convolution fusion | flops 2640445440 | bytes 17342976 | tf_op jit(solution)/shard_map/dot_general | solution.py:28
  626.8 11.3 multiply_reduce_fusion.1
  638.0 12.6 %multiply_convert_fusion.1 = bf16[17,512,512]{1,2,0:T(8,128)(2,1)S(1)} fusion(f32[17,512,512]{1,2,0:T(8,128)} %get-tuple-element.441, f32[17,512]{1,0:T(8,128)S(1)} %get-tuple-element.440, f32[17,512,512]{1,2,0:T(8,128)} %get-tuple-element.436, f32[17,512]{1,0:T(8,128)S(1)} %copy-done.92), kind=kLoop, calls=%fused_computation.4 | loop fusion | flops 17825792 | bytes 44634112 | tf_op jit(solution)/shard_map/convert_element_type | solution.py:219
  712.9 12.0 convolution_convert_fusion.8
  900.3 11.4 multiply_reduce_fusion
  913.9 12.7 %multiply_convert_fusion = bf16[17,512,512]{1,2,0:T(8,128)(2,1)S(1)} fusion(f32[17,512,512]{1,2,0:T(8,128)} %get-tuple-element.447, f32[17,512]{1,0:T(8,128)S(1)} %get-tuple-element.446, f32[17,512,512]{1,2,0:T(8,128)} %get-tuple-element.430, f32[17,512]{1,0:T(8,128)S(1)} %copy-done.90), kind=kLoop, calls=%fused_computation.2 | loop fusion | flops 17825792 | bytes 44634112 | tf_op jit(solution)/shard_map/convert_element_type | solution.py:219
  931.4 11.0 collective-permute-done.55
  1007.3 12.3 %convolution_convert_fusion.4 = bf16[1152,2176]{1,0:T(8,128)(2,1)} fusion(bf16[512,1088]{0,1:T(8,128)(2,1)S(1)} %copy-done.71, bf16[512,1088]{0,1:T(8,128)(2,1)S(1)} %copy-done.70, bf16[512,1152]{1,0:T(8,128)(2,1)} %copy-done.139, bf16[512,1152]{1,0:T(8,128)(2,1)} %get-tuple-element.400), kind=kOutput, calls=%fused_computation.16 | convolution fusion | flops 5158879232 | bytes 9601024 | tf_op jit(solution)/shard_map/dot_general | solution.py:32
  1082.9 13.4 %collective-permute-done.65 = bf16[136,1088]{1,0:T(8,128)(2,1)S(1)} collective-permute-done((bf16[136,1088]{1,0:T(8,128)(2,1)S(1)}, bf16[136,1088]{1,0:T(8,128)(2,1)S(1)}, u32[]{:S(2)}, u32[]{:S(2)}) %collective-permute-start.65) | collective-permute-done | bytes 295968 | tf_op jit(solution)/shard_map/ppermute | solution.py:62
  1107.1 14.1 %collective-permute-done.69 = bf16[72,2176]{1,0:T(8,128)(2,1)S(1)} collective-permute-done((bf16[72,2176]{1,0:T(8,128)(2,1)S(1)}, bf16[72,2176]{1,0:T(8,128)(2,1)S(1)}, u32[]{:S(2)}, u32[]{:S(2)}) %collective-permute-start.69) | collective-permute-done | bytes 313376 | tf_op jit(solution)/shard_map/ppermute | solution.py:62
  1136.7 12.5 %collective-permute-done.73 = bf16[4,72,2176]{2,1,0:T(8,128)(2,1)S(1)} collective-permute-done((bf16[4,72,2176]{2,1,0:T(8,128)(2,1)S(1)}, bf16[4,72,2176]{2,1,0:T(8,128)(2,1)S(1)}, u32[]{:S(2)}, u32[]{:S(2)}) %collective-permute-start.73) | collective-permute-done | bytes 1253408 | tf_op jit(solution)/shard_map/ppermute | solution.py:62
  1168.8 11.5 collective-permute-done.75
  (843 shorter events, 863.9 us)
Async XLA Ops:
  131.9 48.5 %collective-permute-start.15 = (bf16[1152,2176]{1,0:T(8,128)(2,1)}, bf16[1152,2176]{1,0:T(8,128)(2,1)}, u32[]{:S(2)}, u32[]{:S(2)}) collective-permute-start(bf16[1152,2176]{1,0:T(8,128)(2,1)} %bitcast.23), channel_id=1, source_target_pairs={{0,16},{1,17},{2,18},{3,19},{4,20},{5,21},{6,22},{7,23},{8,24},{9,... | collective-permute-start | bytes 15040520 | tf_op jit(solution)/shard_map/ppermute | solution.py:62
  180.4 63.1 %collective-permute-start.26 = (bf16[72,2176]{1,0:T(8,128)(2,1)S(1)}, bf16[72,2176]{1,0:T(8,128)(2,1)S(1)}, u32[]{:S(2)}, u32[]{:S(2)}) collective-permute-start(bf16[72,2176]{1,0:T(8,128)(2,1)S(1)} %get-tuple-element.155), channel_id=1, source_target_pairs={{0,12},{1,13},{2,14},{3,15},{4,0},{5,1},{6,2},{7,3},{8,4},{9,5},{1... | collective-permute-start | bytes 940040 | tf_op jit(solution)/shard_map/ppermute | solution.py:62
  181.2 66.7 %collective-permute-start.25 = (bf16[72,2176]{1,0:T(8,128)(2,1)S(1)}, bf16[72,2176]{1,0:T(8,128)(2,1)S(1)}, u32[]{:S(2)}, u32[]{:S(2)}) collective-permute-start(bf16[72,2176]{1,0:T(8,128)(2,1)S(1)} %get-tuple-element.155), channel_id=1, source_target_pairs={{0,8},{1,9},{2,10},{3,11},{4,12},{5,13},{6,14},{7,15},{8,0},{9,1},... | collective-permute-start | bytes 940040 | tf_op jit(solution)/shard_map/ppermute | solution.py:62
  185.9 71.0 %collective-permute-start.23 = (bf16[4,72,2176]{2,1,0:T(8,128)(2,1)}, bf16[4,72,2176]{2,1,0:T(8,128)(2,1)}, u32[]{:S(2)}, u32[]{:S(2)}) collective-permute-start(bf16[4,72,2176]{2,1,0:T(8,128)(2,1)} %pad_maximum_fusion.17), channel_id=1, source_target_pairs={{0,1},{1,0},{2,3},{3,2},{4,5},{5,4},{6,7},{7,6},{8,9},{9,8},{10,11... | collective-permute-start | bytes 3760136 | tf_op jit(solution)/shard_map/ppermute | solution.py:62
  187.9 72.4 %collective-permute-start.22 = (bf16[2,4,136,1088]{3,2,1,0:T(8,128)(2,1)}, bf16[2,4,136,1088]{3,2,1,0:T(8,128)(2,1)}, u32[]{:S(2)}, u32[]{:S(2)}) collective-permute-start(bf16[2,4,136,1088]{3,2,1,0:T(8,128)(2,1)} %pad_maximum_fusion.8), channel_id=1, source_target_pairs={{0,2},{1,3},{2,0},{3,1},{4,6},{5,7},{6,4},{7,5},{8,10},{9,11},{10,... | collective-permute-start | bytes 7102472 | tf_op jit(solution)/shard_map/ppermute | solution.py:62
  200.4 64.8 %collective-permute-start.21 = (bf16[1152,2176]{1,0:T(8,128)(2,1)}, bf16[1152,2176]{1,0:T(8,128)(2,1)}, u32[]{:S(2)}, u32[]{:S(2)}) collective-permute-start(bf16[1152,2176]{1,0:T(8,128)(2,1)} %bitcast.30), channel_id=1, source_target_pairs={{0,16},{1,17},{2,18},{3,19},{4,20},{5,21},{6,22},{7,23},{8,24},{9,... | collective-permute-start | bytes 15040520 | tf_op jit(solution)/shard_map/ppermute | solution.py:62
  265.2 58.0 %collective-permute-start.32 = (bf16[136,1088]{1,0:T(8,128)(2,1)}, bf16[136,1088]{1,0:T(8,128)(2,1)}, u32[]{:S(2)}, u32[]{:S(2)}) collective-permute-start(bf16[136,1088]{1,0:T(8,128)(2,1)} %get-tuple-element.162), channel_id=1, source_target_pairs={{0,4},{1,5},{2,6},{3,7},{4,8},{5,9},{6,10},{7,11},{8,12},{9,13},{1... | collective-permute-start | bytes 887816 | tf_op jit(solution)/shard_map/ppermute | solution.py:62
  265.2 56.9 %collective-permute-start.31 = (bf16[136,1088]{1,0:T(8,128)(2,1)}, bf16[136,1088]{1,0:T(8,128)(2,1)}, u32[]{:S(2)}, u32[]{:S(2)}) collective-permute-start(bf16[136,1088]{1,0:T(8,128)(2,1)} %get-tuple-element.162), channel_id=1, source_target_pairs={{0,8},{1,9},{2,10},{3,11},{4,12},{5,13},{6,14},{7,15},{8,0},{9,1},... | collective-permute-start | bytes 887816 | tf_op jit(solution)/shard_map/ppermute | solution.py:62
  266.3 53.9 %collective-permute-start.30 = (bf16[136,1088]{1,0:T(8,128)(2,1)}, bf16[136,1088]{1,0:T(8,128)(2,1)}, u32[]{:S(2)}, u32[]{:S(2)}) collective-permute-start(bf16[136,1088]{1,0:T(8,128)(2,1)} %get-tuple-element.162), channel_id=1, source_target_pairs={{0,12},{1,13},{2,14},{3,15},{4,0},{5,1},{6,2},{7,3},{8,4},{9,5},{1... | collective-permute-start | bytes 887816 | tf_op jit(solution)/shard_map/ppermute | solution.py:62
  278.2 51.1 %collective-permute-start.29 = (bf16[4,72,2176]{2,1,0:T(8,128)(2,1)S(1)}, bf16[4,72,2176]{2,1,0:T(8,128)(2,1)}, u32[]{:S(2)}, u32[]{:S(2)}) collective-permute-start(bf16[4,72,2176]{2,1,0:T(8,128)(2,1)S(1)} %pad_maximum_fusion.18), channel_id=1, source_target_pairs={{0,1},{1,0},{2,3},{3,2},{4,5},{5,4},{6,7},{7,6},{8,9},{9,8},{10,11... | collective-permute-start | bytes 3760136 | tf_op jit(solution)/shard_map/ppermute | solution.py:62
  287.2 66.3 %collective-permute-start.27 = (bf16[2176,1088]{0,1:T(8,128)(2,1)}, bf16[2176,1088]{0,1:T(8,128)(2,1)}, u32[]{:S(2)}, u32[]{:S(2)}) collective-permute-start(bf16[2176,1088]{0,1:T(8,128)(2,1)} %copy.295), channel_id=1, source_target_pairs={{0,16},{1,17},{2,18},{3,19},{4,20},{5,21},{6,22},{7,23},{8,24},{9,... | collective-permute-start | bytes 14204936 | tf_op jit(solution)/shard_map/ppermute | solution.py:62
  353.5 49.4 %collective-permute-start.33 = (bf16[1152,2176]{1,0:T(8,128)(2,1)}, bf16[1152,2176]{1,0:T(8,128)(2,1)}, u32[]{:S(2)}, u32[]{:S(2)}) collective-permute-start(bf16[1152,2176]{1,0:T(8,128)(2,1)} %bitcast.65), channel_id=1, source_target_pairs={{0,16},{1,17},{2,18},{3,19},{4,20},{5,21},{6,22},{7,23},{8,24},{9,... | collective-permute-start | bytes 15040520 | tf_op jit(solution)/shard_map/ppermute | solution.py:62
  413.8 50.0 %collective-permute-start.37 = (bf16[2,4,136,1088]{3,2,1,0:T(8,128)(2,1)}, bf16[2,4,136,1088]{3,2,1,0:T(8,128)(2,1)}, u32[]{:S(2)}, u32[]{:S(2)}) collective-permute-start(bf16[2,4,136,1088]{3,2,1,0:T(8,128)(2,1)} %pad_maximum_fusion.11), channel_id=1, source_target_pairs={{0,2},{1,3},{2,0},{3,1},{4,6},{5,7},{6,4},{7,5},{8,10},{9,11},{10,... | collective-permute-start | bytes 7102472 | tf_op jit(solution)/shard_map/ppermute | solution.py:62
  421.1 48.5 %collective-permute-start.36 = (bf16[1152,2176]{1,0:T(8,128)(2,1)}, bf16[1152,2176]{1,0:T(8,128)(2,1)}, u32[]{:S(2)}, u32[]{:S(2)}) collective-permute-start(bf16[1152,2176]{1,0:T(8,128)(2,1)} %bitcast.68), channel_id=1, source_target_pairs={{0,16},{1,17},{2,18},{3,19},{4,20},{5,21},{6,22},{7,23},{8,24},{9,... | collective-permute-start | bytes 15040520 | tf_op jit(solution)/shard_map/ppermute | solution.py:62
  484.7 70.7 %collective-permute-start.38 = (bf16[2176,1088]{0,1:T(8,128)(2,1)}, bf16[2176,1088]{0,1:T(8,128)(2,1)}, u32[]{:S(2)}, u32[]{:S(2)}) collective-permute-start(bf16[2176,1088]{0,1:T(8,128)(2,1)} %copy.305), channel_id=1, source_target_pairs={{0,16},{1,17},{2,18},{3,19},{4,20},{5,21},{6,22},{7,23},{8,24},{9,... | collective-permute-start | bytes 14204936 | tf_op jit(solution)/shard_map/ppermute | solution.py:62
  696.8 48.5 %collective-permute-start.43 = (bf16[4,136,1088]{2,1,0:T(8,128)(2,1)}, bf16[4,136,1088]{2,1,0:T(8,128)(2,1)}, u32[]{:S(2)}, u32[]{:S(2)}) collective-permute-start(bf16[4,136,1088]{2,1,0:T(8,128)(2,1)} %get-tuple-element.189), channel_id=1, source_target_pairs={{0,1},{1,0},{2,3},{3,2},{4,5},{5,4},{6,7},{7,6},{8,9},{9,8},{10,11... | collective-permute-start | bytes 3551240 | tf_op jit(solution)/shard_map/ppermute | solution.py:62
  752.2 55.2 %collective-permute-start.48 = (bf16[4,72,2176]{2,1,0:T(8,128)(2,1)}, bf16[4,72,2176]{2,1,0:T(8,128)(2,1)}, u32[]{:S(2)}, u32[]{:S(2)}) collective-permute-start(bf16[4,72,2176]{2,1,0:T(8,128)(2,1)} %get-tuple-element.195), channel_id=1, source_target_pairs={{0,1},{1,0},{2,3},{3,2},{4,5},{5,4},{6,7},{7,6},{8,9},{9,8},{10,11... | collective-permute-start | bytes 3760136 | tf_op jit(solution)/shard_map/ppermute | solution.py:62
  753.7 55.3 %collective-permute-start.49 = (bf16[16,72,2176]{2,1,0:T(8,128)(2,1)}, bf16[16,72,2176]{2,1,0:T(8,128)(2,1)}, u32[]{:S(2)}, u32[]{:S(2)}) collective-permute-start(bf16[16,72,2176]{2,1,0:T(8,128)(2,1)} %get-tuple-element.197), channel_id=1, source_target_pairs={{0,16},{1,17},{2,18},{3,19},{4,20},{5,21},{6,22},{7,23},{8,24},{9,... | collective-permute-start | bytes 15040520 | tf_op jit(solution)/shard_map/ppermute | solution.py:62
  985.7 55.8 %collective-permute-start.58 = (bf16[72,2176]{1,0:T(8,128)(2,1)}, bf16[72,2176]{1,0:T(8,128)(2,1)S(1)}, u32[]{:S(2)}, u32[]{:S(2)}) collective-permute-start(bf16[72,2176]{1,0:T(8,128)(2,1)} %get-tuple-element.391), channel_id=1, source_target_pairs={{0,12},{1,13},{2,14},{3,15},{4,0},{5,1},{6,2},{7,3},{8,4},{9,5},{1... | collective-permute-start | bytes 940040 | tf_op jit(solution)/shard_map/ppermute | solution.py:62
  989.2 52.4 %collective-permute-start.60 = (bf16[72,2176]{1,0:T(8,128)(2,1)}, bf16[72,2176]{1,0:T(8,128)(2,1)}, u32[]{:S(2)}, u32[]{:S(2)}) collective-permute-start(bf16[72,2176]{1,0:T(8,128)(2,1)} %get-tuple-element.392), channel_id=1, source_target_pairs={{0,4},{1,5},{2,6},{3,7},{4,8},{5,9},{6,10},{7,11},{8,12},{9,13},{1... | collective-permute-start | bytes 940040 | tf_op jit(solution)/shard_map/ppermute | solution.py:62
  989.2 53.1 %collective-permute-start.59 = (bf16[72,2176]{1,0:T(8,128)(2,1)S(1)}, bf16[72,2176]{1,0:T(8,128)(2,1)}, u32[]{:S(2)}, u32[]{:S(2)}) collective-permute-start(bf16[72,2176]{1,0:T(8,128)(2,1)S(1)} %get-tuple-element.393), channel_id=1, source_target_pairs={{0,8},{1,9},{2,10},{3,11},{4,12},{5,13},{6,14},{7,15},{8,0},{9,1},... | collective-permute-start | bytes 940040 | tf_op jit(solution)/shard_map/ppermute | solution.py:62
  989.7 53.9 %collective-permute-start.61 = (bf16[4,136,1088]{2,1,0:T(8,128)(2,1)}, bf16[4,136,1088]{2,1,0:T(8,128)(2,1)}, u32[]{:S(2)}, u32[]{:S(2)}) collective-permute-start(bf16[4,136,1088]{2,1,0:T(8,128)(2,1)} %get-tuple-element.218), channel_id=1, source_target_pairs={{0,1},{1,0},{2,3},{3,2},{4,5},{5,4},{6,7},{7,6},{8,9},{9,8},{10,11... | collective-permute-start | bytes 3551240 | tf_op jit(solution)/shard_map/ppermute | solution.py:62
  993.9 52.4 %collective-permute-start.62 = (bf16[2,4,72,2176]{3,2,1,0:T(8,128)(2,1)}, bf16[2,4,72,2176]{3,2,1,0:T(8,128)(2,1)}, u32[]{:S(2)}, u32[]{:S(2)}) collective-permute-start(bf16[2,4,72,2176]{3,2,1,0:T(8,128)(2,1)} %bitcast.147), channel_id=1, source_target_pairs={{0,2},{1,3},{2,0},{3,1},{4,6},{5,7},{6,4},{7,5},{8,10},{9,11},{10,... | collective-permute-start | bytes 7520264 | tf_op jit(solution)/shard_map/ppermute | solution.py:62
  1050.0 46.8 %collective-permute-start.68 = (bf16[16,72,2176]{2,1,0:T(8,128)(2,1)}, bf16[16,72,2176]{2,1,0:T(8,128)(2,1)}, u32[]{:S(2)}, u32[]{:S(2)}) collective-permute-start(bf16[16,72,2176]{2,1,0:T(8,128)(2,1)} %get-tuple-element.230), channel_id=1, source_target_pairs={{0,16},{1,17},{2,18},{3,19},{4,20},{5,21},{6,22},{7,23},{8,24},{9,... | collective-permute-start | bytes 15040520 | tf_op jit(solution)/shard_map/ppermute | solution.py:62
  (224 other events, 4880.8 us)

commit v4 on v3

--- a/solution.py
+++ b/solution.py
@@ -54,9 +54,15 @@
         self.swap = pairs(lambda c, d: (1 - c) * count + d)
         self.first = pairs(lambda c, d: c * count + (d ^ (2 if c == 0 else 1)))
         self.second = pairs(lambda c, d: c * count + (d ^ (1 if c == 0 else 2)))
-        self.turns = [
-            pairs(lambda c, d, k=k: c * count + (d + 4 * k) % count) for k in range(self.deep)
-        ]
+        self.levels = {
+            k: pairs(lambda c, d, k=k: c * count + (d ^ (4 * k)) % count) for k in (1, 2)
+        }
+
+    def by_level(self, x):
+        shape = x.shape
+        x = x.reshape((2, 2) + shape[1:])
+        x = jnp.where(self.level // 2 == 1, x[::-1], x)
+        return jnp.where(self.level % 2 == 1, x[:, ::-1], x).reshape(shape)
 
     def send(self, x, perm):
         return lax.ppermute(x, BOTH, perm)
@@ -72,7 +78,7 @@
         if not self.staged:
             return jnp.arange(self.count)
         quads = self.quad ^ jnp.stack([jnp.int32(v) for v in self.flips(core)])
-        levels = (self.level - jnp.arange(self.deep)) % self.deep
+        levels = self.level ^ jnp.arange(self.deep)
         return (levels[None, :] * 4 + quads[:, None]).reshape(-1)
 
 
@@ -87,13 +93,9 @@
         links, (half,) = self.links, self.live
         if not links.staged:
             return
-        deep = links.deep
-        turned = [half] + [links.send(half, links.turns[k]) for k in range(1, deep)]
-        if self.sorted:
-            listed = jnp.stack([turned[(-t) % deep] for t in range(2 * deep)])
-            self.live = [lax.dynamic_slice_in_dim(listed, deep - links.level, deep, 0)]
-        else:
-            self.live = [jnp.stack(turned)]
+        pair = jnp.stack([half, links.send(half, links.levels[1])])
+        turned = jnp.concatenate([pair, links.send(pair, links.levels[2])], axis=0)
+        self.live = [links.by_level(turned) if self.sorted else turned]
 
     def stage_second(self):
         if self.links.staged:
@@ -164,17 +166,11 @@
     def stage_turn(self):
         links, (kept,) = self.links, self.live
         if links.staged:
-            deep = links.deep
-
-            def block(step):
-                if not self.sorted:
-                    return kept[step]
-                place = (links.level + deep - step) % deep
-                return lax.dynamic_slice_in_dim(kept, place, 1, 0)[0]
-
-            result = block(0).astype(F32)
-            for k in range(1, deep):
-                result = result + links.send(block(k), links.turns[deep - k]).astype(F32)
+            if self.sorted:
+                kept = links.by_level(kept)
+            arrived = links.send(kept[2:], links.levels[2])
+            pair = kept[:2].astype(F32) + arrived.astype(F32)
+            result = pair[0] + links.send(pair[1].astype(BF16), links.levels[1]).astype(F32)
             self.live = [result]
 
 
@@ -352,7 +348,7 @@
         return (s["hidden"] + (total + s["shifts"][5])).astype(BF16)
 
     def advance(jobs, slot, stages):
-        for back, stage in enumerate(stages):
+        for back, stage in reversed(list(enumerate(stages))):
             if 0 <= slot - back < len(jobs):
                 getattr(jobs[slot - back], stage)()
 
@@ -454,9 +450,10 @@
     begun = []
 
     def advance_back(slot):
-        for job, start in zip(reduces, begun):
-            if 1 <= slot - start < 5:
-                getattr(job, returning[slot - start])()
+        for back in range(1, 5):
+            for job, start in zip(reduces, begun):
+                if slot - start == back:
+                    getattr(job, returning[back])()
 
     def turn_back(slot, result):
         job, out = result

time: 1220 us -> 1270 us (1.041)
  waiting for transfers between devices: 274 us -> 352 us
  starting transfers between devices: 94.5 us -> 63 us
    ppermute x80 -> x68, waiting for transfers between devices: 274 us -> 352 us  [send(): return lax.ppermute(x, BOTH, perm)]
    ppermute x80 -> x68, starting transfers between devices: 94.5 us -> 63 us  [send(): return lax.ppermute(x, BOTH, perm)]
  transfers between devices with their start and end apart: 80 -> 68, of which waited for: 28 -> 28; matrix products, arithmetic and copies ran while one was open for 51% -> 48% of each run, Pallas kernels for 0% -> 0%
where the time goes in v4:
time: 1270 us; the launch traced here: 1250 us
  matrix products  476 us (37%)
  waiting for transfers between devices  352 us (28%)
  other arithmetic  214 us (17%)
  local copies, waits for them, and re-layouts  145 us (11%)
  starting transfers between devices  63 us (5%)
    ppermute x68, waiting for transfers between devices, send(): return lax.ppermute(x, BOTH, perm)  352 us
    dot_general x26, matrix products, product(): return jnp.dot(left, right, preferred_element_type=F32)  152 us
    dot_general x30, matrix products, against(): lax.dot_general(left, right, (((1,), (1,)), ((), ())), preferred_element_...  138 us
    dot_general x14, matrix products, outer_sum(): lax.dot_general(left, right, (((0,), (0,)), ((), ())), preferred_element_...  86.9 us
    ppermute x68, starting transfers between devices, send(): return lax.ppermute(x, BOTH, perm)  63 us
    convert_element_type x6, other arithmetic, stage_swap(): (keep.astype(F32) + self.links.swap_cores(away).astype(F32)).astype(BF16)  37.4 us
    convert_element_type x4, local copies, waits for them, and re-layouts, backward_down(): outer_sum(s['active'][i], grad_rows).astype(BF16)  33.5 us
    sub x2, matrix products, attend(): expo_vals = jnp.exp(masked - row_top)  29.5 us
  transfers between devices with their start and end apart: 68, of which 28 were waited for; matrix products, arithmetic and copies ran while one was open for 48% of the time, Pallas kernels for 0%

profile of v4, /device:TPU:0, one launch (start us, length us, event | category | flops | bytes accessed | tf_op | source)
XLA Modules:
  0.0 1253.7 jit_solution(9624337939383426571)
XLA Ops:
  29.3 27.4 %collective-permute-done.2 = bf16[2,72,2176]{2,1,0:T(8,128)(2,1)S(1)} collective-permute-done((bf16[2,72,2176]{2,1,0:T(8,128)(2,1)S(1)}, bf16[2,72,2176]{2,1,0:T(8,128)(2,1)S(1)}, u32[]{:S(2)}, u32[]{:S(2)}) %collective-permute-start.2) | collective-permute-done | bytes 626720 | tf_op jit(solution)/shard_map/ppermute | solution.py:68
  68.6 27.2 %collective-permute-done.7 = bf16[2,72,2176]{2,1,0:T(8,128)(2,1)S(1)} collective-permute-done((bf16[2,72,2176]{2,1,0:T(8,128)(2,1)S(1)}, bf16[2,72,2176]{2,1,0:T(8,128)(2,1)S(1)}, u32[]{:S(2)}, u32[]{:S(2)}) %collective-permute-start.7) | collective-permute-done | bytes 626720 | tf_op jit(solution)/shard_map/ppermute | solution.py:68
  111.9 26.1 %collective-permute-done.11 = bf16[2,136,1088]{2,1,0:T(8,128)(2,1)} collective-permute-done((bf16[2,136,1088]{2,1,0:T(8,128)(2,1)}, bf16[2,136,1088]{2,1,0:T(8,128)(2,1)}, u32[]{:S(2)}, u32[]{:S(2)}) %collective-permute-start.11) | collective-permute-done | bytes 591904 | tf_op jit(solution)/shard_map/ppermute | solution.py:68
  165.0 26.3 %collective-permute-done.16 = bf16[2,72,2176]{2,1,0:T(8,128)(2,1)S(1)} collective-permute-done((bf16[2,72,2176]{2,1,0:T(8,128)(2,1)S(1)}, bf16[2,72,2176]{2,1,0:T(8,128)(2,1)S(1)}, u32[]{:S(2)}, u32[]{:S(2)}) %collective-permute-start.16) | collective-permute-done | bytes 626720 | tf_op jit(solution)/shard_map/ppermute | solution.py:68
  223.2 19.0 %fusion.384 = (f32[17,512]{1,0:T(8,128)S(1)}, f32[17,512,512]{1,2,0:T(8,128)}) fusion(bf16[512,17,64]{0,2,1:T(8,128)(2,1)S(1)} %bitcast.461, bf16[512,17,64]{0,2,1:T(8,128)(2,1)S(1)} %bitcast.429, pred[512,512]{0,1:T(8,128)(4,1)S(1)} %copy-done.87), kind=kOutput, calls=%fused_computation.704 | convolution fusion | flops 588251648 | bytes 20350976 | tf_op jit(solution)/shard_map/sub | solution.py:196
  271.4 23.7 %collective-permute-done.21 = bf16[2,72,2176]{2,1,0:T(8,128)(2,1)S(1)} collective-permute-done((bf16[2,72,2176]{2,1,0:T(8,128)(2,1)S(1)}, bf16[2,72,2176]{2,1,0:T(8,128)(2,1)S(1)}, u32[]{:S(2)}, u32[]{:S(2)}) %collective-permute-start.21) | collective-permute-done | bytes 626720 | tf_op jit(solution)/shard_map/ppermute | solution.py:68
  319.1 17.1 %multiply_convert_fusion.5 = (bf16[512,2176]{1,0:T(8,128)(2,1)}, f32[512,2176]{1,0:T(8,128)}, f32[512,2176]{1,0:T(8,128)}) fusion(f32[2176]{0:T(1024)S(1)} %select_n.589, bf16[512,1152]{1,0:T(8,128)(2,1)} %fusion.137, bf16[1152,2176]{1,0:T(8,128)(2,1)} %bitcast.24), kind=kOutput, calls=%fused_computation.168 | convolution fusion | flops 2640445440 | bytes 17342976 | tf_op jit(solution)/shard_map/dot_general | solution.py:28
  341.0 16.2 %multiply_convert_fusion.4 = (bf16[512,2176]{1,0:T(8,128)(2,1)}, f32[512,2176]{1,0:T(8,128)}, f32[512,2176]{1,0:T(8,128)}) fusion(f32[2176]{0:T(1024)S(1)} %select_n.591, bf16[512,1152]{1,0:T(8,128)(2,1)S(1)} %fusion.133, bf16[1152,2176]{1,0:T(8,128)(2,1)} %collective-permute-done.17), kind=kOutput, calls=%fused_computation.155 | convolution fusion | flops 2640445440 | bytes 17342976 | tf_op jit(solution)/shard_map/dot_general | solution.py:28
  357.2 12.0 collective-permute-done.26
  397.4 18.2 %collective-permute-done.29 = bf16[4,136,1088]{2,1,0:T(8,128)(2,1)S(1)} collective-permute-done((bf16[4,136,1088]{2,1,0:T(8,128)(2,1)}, bf16[4,136,1088]{2,1,0:T(8,128)(2,1)S(1)}, u32[]{:S(2)}, u32[]{:S(2)}) %collective-permute-start.29) | collective-permute-done | bytes 1183776 | tf_op jit(solution)/shard_map/ppermute | solution.py:68
  457.1 10.5 fusion.385
  513.7 16.5 %multiply_convert_fusion.3 = (bf16[512,2176]{1,0:T(8,128)(2,1)S(1)}, f32[512,2176]{1,0:T(8,128)}, f32[512,2176]{1,0:T(8,128)}) fusion(f32[2176]{0:T(1024)S(1)} %select_n.598, bf16[512,1152]{1,0:T(8,128)(2,1)} %fusion.139, bf16[1152,2176]{1,0:T(8,128)(2,1)} %bitcast.436), kind=kOutput, calls=%fused_computation.138 | convolution fusion | flops 2640445440 | bytes 17342976 | tf_op jit(solution)/shard_map/dot_general | solution.py:28
  544.2 16.4 %multiply_convert_fusion.2 = (bf16[512,2176]{1,0:T(8,128)(2,1)S(1)}, f32[512,2176]{1,0:T(8,128)}, f32[512,2176]{1,0:T(8,128)}) fusion(f32[2176]{0:T(1024)S(1)} %select_n.600, bf16[512,1152]{1,0:T(8,128)(2,1)} %fusion.135, bf16[1152,2176]{1,0:T(8,128)(2,1)} %collective-permute-done.30), kind=kOutput, calls=%fused_computation.125 | convolution fusion | flops 2640445440 | bytes 17342976 | tf_op jit(solution)/shard_map/dot_general | solution.py:28
  659.2 11.3 multiply_reduce_fusion.1
  670.4 12.6 %multiply_convert_fusion.1 = bf16[17,512,512]{1,2,0:T(8,128)(2,1)S(1)} fusion(f32[17,512,512]{1,2,0:T(8,128)} %get-tuple-element.423, f32[17,512]{1,0:T(8,128)S(1)} %get-tuple-element.422, f32[17,512,512]{1,2,0:T(8,128)} %get-tuple-element.418, f32[17,512]{1,0:T(8,128)S(1)} %copy-done.99), kind=kLoop, calls=%fused_computation.4 | loop fusion | flops 17825792 | bytes 44634112 | tf_op jit(solution)/shard_map/convert_element_type | solution.py:215
  745.2 12.4 convolution_convert_fusion.8
  935.5 11.4 multiply_reduce_fusion
  949.5 12.7 %multiply_convert_fusion = bf16[17,512,512]{1,2,0:T(8,128)(2,1)S(1)} fusion(f32[17,512,512]{1,2,0:T(8,128)} %get-tuple-element.429, f32[17,512]{1,0:T(8,128)S(1)} %get-tuple-element.428, f32[17,512,512]{1,2,0:T(8,128)} %get-tuple-element.412, f32[17,512]{1,0:T(8,128)S(1)} %copy-done.97), kind=kLoop, calls=%fused_computation.2 | loop fusion | flops 17825792 | bytes 44634112 | tf_op jit(solution)/shard_map/convert_element_type | solution.py:215
  967.0 10.6 collective-permute-done.47
  1039.2 11.8 convolution_convert_fusion.4
  1095.3 21.3 %collective-permute-done.55 = bf16[2,136,1088]{2,1,0:T(8,128)(2,1)S(1)} collective-permute-done((bf16[2,136,1088]{2,1,0:T(8,128)(2,1)}, bf16[2,136,1088]{2,1,0:T(8,128)(2,1)S(1)}, u32[]{:S(2)}, u32[]{:S(2)}) %collective-permute-start.55) | collective-permute-done | bytes 591904 | tf_op jit(solution)/shard_map/ppermute | solution.py:68
  1135.0 27.4 %collective-permute-done.59 = bf16[2,72,2176]{2,1,0:T(8,128)(2,1)S(1)} collective-permute-done((bf16[2,72,2176]{2,1,0:T(8,128)(2,1)S(1)}, bf16[2,72,2176]{2,1,0:T(8,128)(2,1)S(1)}, u32[]{:S(2)}, u32[]{:S(2)}) %collective-permute-start.59) | collective-permute-done | bytes 626720 | tf_op jit(solution)/shard_map/ppermute | solution.py:68
  1177.0 12.8 %collective-permute-done.62 = bf16[4,72,2176]{2,1,0:T(8,128)(2,1)S(1)} collective-permute-done((bf16[4,72,2176]{2,1,0:T(8,128)(2,1)S(1)}, bf16[4,72,2176]{2,1,0:T(8,128)(2,1)S(1)}, u32[]{:S(2)}, u32[]{:S(2)}) %collective-permute-start.62) | collective-permute-done | bytes 1253408 | tf_op jit(solution)/shard_map/ppermute | solution.py:68
  1193.5 27.4 %collective-permute-done.63 = bf16[2,72,2176]{2,1,0:T(8,128)(2,1)S(1)} collective-permute-done((bf16[2,72,2176]{2,1,0:T(8,128)(2,1)S(1)}, bf16[2,72,2176]{2,1,0:T(8,128)(2,1)S(1)}, u32[]{:S(2)}, u32[]{:S(2)}) %collective-permute-start.63) | collective-permute-done | bytes 626720 | tf_op jit(solution)/shard_map/ppermute | solution.py:68
  (835 shorter events, 821.5 us)
Async XLA Ops:
  98.6 44.2 %collective-permute-start.8 = (bf16[2,4,72,2176]{3,2,1,0:T(8,128)(2,1)}, bf16[2,4,72,2176]{3,2,1,0:T(8,128)(2,1)}, u32[]{:S(2)}, u32[]{:S(2)}) collective-permute-start(bf16[2,4,72,2176]{3,2,1,0:T(8,128)(2,1)} %pad_maximum_fusion.6), channel_id=1, source_target_pairs={{0,2},{1,3},{2,0},{3,1},{4,6},{5,7},{6,4},{7,5},{8,10},{9,11},{10,... | collective-permute-start | bytes 7520264 | tf_op jit(solution)/shard_map/ppermute | solution.py:68
  147.9 50.8 %collective-permute-start.12 = (bf16[1152,2176]{1,0:T(8,128)(2,1)}, bf16[1152,2176]{1,0:T(8,128)(2,1)}, u32[]{:S(2)}, u32[]{:S(2)}) collective-permute-start(bf16[1152,2176]{1,0:T(8,128)(2,1)} %bitcast.19), channel_id=1, source_target_pairs={{0,16},{1,17},{2,18},{3,19},{4,20},{5,21},{6,22},{7,23},{8,24},{9,... | collective-permute-start | bytes 15040520 | tf_op jit(solution)/shard_map/ppermute | solution.py:68
  148.1 46.2 %collective-permute-start.13 = (bf16[2,4,72,2176]{3,2,1,0:T(8,128)(2,1)S(1)}, bf16[2,4,72,2176]{3,2,1,0:T(8,128)(2,1)}, u32[]{:S(2)}, u32[]{:S(2)}) collective-permute-start(bf16[2,4,72,2176]{3,2,1,0:T(8,128)(2,1)S(1)} %pad_maximum_fusion.7), channel_id=1, source_target_pairs={{0,2},{1,3},{2,0},{3,1},{4,6},{5,7},{6,4},{7,5},{8,10},{9,11},{10,... | collective-permute-start | bytes 7520264 | tf_op jit(solution)/shard_map/ppermute | solution.py:68
  202.1 61.4 %collective-permute-start.20 = (bf16[72,2176]{1,0:T(8,128)(2,1)S(1)}, bf16[72,2176]{1,0:T(8,128)(2,1)S(1)}, u32[]{:S(2)}, u32[]{:S(2)}) collective-permute-start(bf16[72,2176]{1,0:T(8,128)(2,1)S(1)} %get-tuple-element.155), channel_id=1, source_target_pairs={{0,4},{1,5},{2,6},{3,7},{4,0},{5,1},{6,2},{7,3},{8,12},{9,13},{10,... | collective-permute-start | bytes 940040 | tf_op jit(solution)/shard_map/ppermute | solution.py:68
  202.1 94.2 %collective-permute-start.19 = (bf16[4,72,2176]{2,1,0:T(8,128)(2,1)}, bf16[4,72,2176]{2,1,0:T(8,128)(2,1)}, u32[]{:S(2)}, u32[]{:S(2)}) collective-permute-start(bf16[4,72,2176]{2,1,0:T(8,128)(2,1)} %pad_maximum_fusion.18), channel_id=1, source_target_pairs={{0,1},{1,0},{2,3},{3,2},{4,5},{5,4},{6,7},{7,6},{8,9},{9,8},{10,11... | collective-permute-start | bytes 3760136 | tf_op jit(solution)/shard_map/ppermute | solution.py:68
  202.6 97.0 %collective-permute-start.18 = (bf16[2,4,136,1088]{3,2,1,0:T(8,128)(2,1)}, bf16[2,4,136,1088]{3,2,1,0:T(8,128)(2,1)}, u32[]{:S(2)}, u32[]{:S(2)}) collective-permute-start(bf16[2,4,136,1088]{3,2,1,0:T(8,128)(2,1)} %pad_maximum_fusion.8), channel_id=1, source_target_pairs={{0,2},{1,3},{2,0},{3,1},{4,6},{5,7},{6,4},{7,5},{8,10},{9,11},{10,... | collective-permute-start | bytes 7102472 | tf_op jit(solution)/shard_map/ppermute | solution.py:68
  215.6 88.9 %collective-permute-start.17 = (bf16[1152,2176]{1,0:T(8,128)(2,1)}, bf16[1152,2176]{1,0:T(8,128)(2,1)}, u32[]{:S(2)}, u32[]{:S(2)}) collective-permute-start(bf16[1152,2176]{1,0:T(8,128)(2,1)} %bitcast.24), channel_id=1, source_target_pairs={{0,16},{1,17},{2,18},{3,19},{4,20},{5,21},{6,22},{7,23},{8,24},{9,... | collective-permute-start | bytes 15040520 | tf_op jit(solution)/shard_map/ppermute | solution.py:68
  309.0 61.9 %collective-permute-start.24 = (bf16[4,72,2176]{2,1,0:T(8,128)(2,1)}, bf16[4,72,2176]{2,1,0:T(8,128)(2,1)}, u32[]{:S(2)}, u32[]{:S(2)}) collective-permute-start(bf16[4,72,2176]{2,1,0:T(8,128)(2,1)} %pad_maximum_fusion.19), channel_id=1, source_target_pairs={{0,1},{1,0},{2,3},{3,2},{4,5},{5,4},{6,7},{7,6},{8,9},{9,8},{10,11... | collective-permute-start | bytes 3760136 | tf_op jit(solution)/shard_map/ppermute | solution.py:68
  310.3 64.0 %collective-permute-start.23 = (bf16[2,4,72,2176]{3,2,1,0:T(8,128)(2,1)}, bf16[2,4,72,2176]{3,2,1,0:T(8,128)(2,1)}, u32[]{:S(2)}, u32[]{:S(2)}) collective-permute-start(bf16[2,4,72,2176]{3,2,1,0:T(8,128)(2,1)} %pad_maximum_fusion.9), channel_id=1, source_target_pairs={{0,2},{1,3},{2,0},{3,1},{4,6},{5,7},{6,4},{7,5},{8,10},{9,11},{10,... | collective-permute-start | bytes 7520264 | tf_op jit(solution)/shard_map/ppermute | solution.py:68
  319.1 60.5 %collective-permute-start.22 = (bf16[2176,1088]{0,1:T(8,128)(2,1)}, bf16[2176,1088]{0,1:T(8,128)(2,1)S(1)}, u32[]{:S(2)}, u32[]{:S(2)}) collective-permute-start(bf16[2176,1088]{0,1:T(8,128)(2,1)} %copy.293), channel_id=1, source_target_pairs={{0,16},{1,17},{2,18},{3,19},{4,20},{5,21},{6,22},{7,23},{8,24},{9,... | collective-permute-start | bytes 14204936 | tf_op jit(solution)/shard_map/ppermute | solution.py:68
  379.6 51.5 %collective-permute-start.27 = (bf16[1152,2176]{1,0:T(8,128)(2,1)}, bf16[1152,2176]{1,0:T(8,128)(2,1)}, u32[]{:S(2)}, u32[]{:S(2)}) collective-permute-start(bf16[1152,2176]{1,0:T(8,128)(2,1)} %bitcast.56), channel_id=1, source_target_pairs={{0,16},{1,17},{2,18},{3,19},{4,20},{5,21},{6,22},{7,23},{8,24},{9,... | collective-permute-start | bytes 15040520 | tf_op jit(solution)/shard_map/ppermute | solution.py:68
  381.8 44.2 %collective-permute-start.28 = (bf16[2,4,72,2176]{3,2,1,0:T(8,128)(2,1)}, bf16[2,4,72,2176]{3,2,1,0:T(8,128)(2,1)}, u32[]{:S(2)}, u32[]{:S(2)}) collective-permute-start(bf16[2,4,72,2176]{3,2,1,0:T(8,128)(2,1)} %pad_maximum_fusion.10), channel_id=1, source_target_pairs={{0,2},{1,3},{2,0},{3,1},{4,6},{5,7},{6,4},{7,5},{8,10},{9,11},{10,... | collective-permute-start | bytes 7520264 | tf_op jit(solution)/shard_map/ppermute | solution.py:68
  441.6 50.8 %collective-permute-start.31 = (bf16[2,4,136,1088]{3,2,1,0:T(8,128)(2,1)}, bf16[2,4,136,1088]{3,2,1,0:T(8,128)(2,1)}, u32[]{:S(2)}, u32[]{:S(2)}) collective-permute-start(bf16[2,4,136,1088]{3,2,1,0:T(8,128)(2,1)} %pad_maximum_fusion.11), channel_id=1, source_target_pairs={{0,2},{1,3},{2,0},{3,1},{4,6},{5,7},{6,4},{7,5},{8,10},{9,11},{10,... | collective-permute-start | bytes 7102472 | tf_op jit(solution)/shard_map/ppermute | solution.py:68
  449.5 48.6 %collective-permute-start.30 = (bf16[1152,2176]{1,0:T(8,128)(2,1)}, bf16[1152,2176]{1,0:T(8,128)(2,1)}, u32[]{:S(2)}, u32[]{:S(2)}) collective-permute-start(bf16[1152,2176]{1,0:T(8,128)(2,1)} %bitcast.435), channel_id=1, source_target_pairs={{0,16},{1,17},{2,18},{3,19},{4,20},{5,21},{6,22},{7,23},{8,24},{9,... | collective-permute-start | bytes 15040520 | tf_op jit(solution)/shard_map/ppermute | solution.py:68
  513.2 70.6 %collective-permute-start.32 = (bf16[2176,1088]{0,1:T(8,128)(2,1)}, bf16[2176,1088]{0,1:T(8,128)(2,1)}, u32[]{:S(2)}, u32[]{:S(2)}) collective-permute-start(bf16[2176,1088]{0,1:T(8,128)(2,1)} %copy.302), channel_id=1, source_target_pairs={{0,16},{1,17},{2,18},{3,19},{4,20},{5,21},{6,22},{7,23},{8,24},{9,... | collective-permute-start | bytes 14204936 | tf_op jit(solution)/shard_map/ppermute | solution.py:68
  657.6 44.1 %collective-permute-start.35 = (bf16[2,4,136,1088]{3,2,1,0:T(8,128)(2,1)}, bf16[2,4,136,1088]{3,2,1,0:T(8,128)(2,1)}, u32[]{:S(2)}, u32[]{:S(2)}) collective-permute-start(bf16[2,4,136,1088]{3,2,1,0:T(8,128)(2,1)} %pad_maximum_fusion.12), channel_id=1, source_target_pairs={{0,2},{1,3},{2,0},{3,1},{4,6},{5,7},{6,4},{7,5},{8,10},{9,11},{10,... | collective-permute-start | bytes 7102472 | tf_op jit(solution)/shard_map/ppermute | solution.py:68
  658.2 47.3 %collective-permute-start.36 = (bf16[16,72,2176]{2,1,0:T(8,128)(2,1)}, bf16[16,72,2176]{2,1,0:T(8,128)(2,1)}, u32[]{:S(2)}, u32[]{:S(2)}) collective-permute-start(bf16[16,72,2176]{2,1,0:T(8,128)(2,1)} %bitcast.509), channel_id=1, source_target_pairs={{0,16},{1,17},{2,18},{3,19},{4,20},{5,21},{6,22},{7,23},{8,24},{9,... | collective-permute-start | bytes 15040520 | tf_op jit(solution)/shard_map/ppermute | solution.py:68
  729.2 49.0 %collective-permute-start.37 = (bf16[4,136,1088]{2,1,0:T(8,128)(2,1)}, bf16[4,136,1088]{2,1,0:T(8,128)(2,1)}, u32[]{:S(2)}, u32[]{:S(2)}) collective-permute-start(bf16[4,136,1088]{2,1,0:T(8,128)(2,1)} %get-tuple-element.189), channel_id=1, source_target_pairs={{0,1},{1,0},{2,3},{3,2},{4,5},{5,4},{6,7},{7,6},{8,9},{9,8},{10,11... | collective-permute-start | bytes 3551240 | tf_op jit(solution)/shard_map/ppermute | solution.py:68
  733.3 46.6 %collective-permute-start.38 = (bf16[2,4,72,2176]{3,2,1,0:T(8,128)(2,1)}, bf16[2,4,72,2176]{3,2,1,0:T(8,128)(2,1)}, u32[]{:S(2)}, u32[]{:S(2)}) collective-permute-start(bf16[2,4,72,2176]{3,2,1,0:T(8,128)(2,1)} %bitcast.97), channel_id=1, source_target_pairs={{0,2},{1,3},{2,0},{3,1},{4,6},{5,7},{6,4},{7,5},{8,10},{9,11},{10,... | collective-permute-start | bytes 7520264 | tf_op jit(solution)/shard_map/ppermute | solution.py:68
  787.8 51.3 %collective-permute-start.41 = (bf16[4,72,2176]{2,1,0:T(8,128)(2,1)}, bf16[4,72,2176]{2,1,0:T(8,128)(2,1)}, u32[]{:S(2)}, u32[]{:S(2)}) collective-permute-start(bf16[4,72,2176]{2,1,0:T(8,128)(2,1)} %get-tuple-element.195), channel_id=1, source_target_pairs={{0,1},{1,0},{2,3},{3,2},{4,5},{5,4},{6,7},{7,6},{8,9},{9,8},{10,11... | collective-permute-start | bytes 3760136 | tf_op jit(solution)/shard_map/ppermute | solution.py:68
  949.4 43.8 %collective-permute-start.49 = (bf16[16,72,2176]{2,1,0:T(8,128)(2,1)}, bf16[16,72,2176]{2,1,0:T(8,128)(2,1)}, u32[]{:S(2)}, u32[]{:S(2)}) collective-permute-start(bf16[16,72,2176]{2,1,0:T(8,128)(2,1)} %bitcast.508), channel_id=1, source_target_pairs={{0,16},{1,17},{2,18},{3,19},{4,20},{5,21},{6,22},{7,23},{8,24},{9,... | collective-permute-start | bytes 15040520 | tf_op jit(solution)/shard_map/ppermute | solution.py:68
  1020.7 47.8 %collective-permute-start.50 = (bf16[2,72,2176]{2,1,0:T(8,128)(2,1)}, bf16[2,72,2176]{2,1,0:T(8,128)(2,1)}, u32[]{:S(2)}, u32[]{:S(2)}) collective-permute-start(bf16[2,72,2176]{2,1,0:T(8,128)(2,1)} %slice.535), channel_id=1, source_target_pairs={{0,8},{1,9},{2,10},{3,11},{4,12},{5,13},{6,14},{7,15},{8,0},{9,1},... | collective-permute-start | bytes 1880072 | tf_op jit(solution)/shard_map/ppermute | solution.py:68
  1022.9 57.3 %collective-permute-start.52 = (bf16[4,136,1088]{2,1,0:T(8,128)(2,1)}, bf16[4,136,1088]{2,1,0:T(8,128)(2,1)}, u32[]{:S(2)}, u32[]{:S(2)}) collective-permute-start(bf16[4,136,1088]{2,1,0:T(8,128)(2,1)} %get-tuple-element.218), channel_id=1, source_target_pairs={{0,1},{1,0},{2,3},{3,2},{4,5},{5,4},{6,7},{7,6},{8,9},{9,8},{10,11... | collective-permute-start | bytes 3551240 | tf_op jit(solution)/shard_map/ppermute | solution.py:68
  1027.6 54.4 %collective-permute-start.53 = (bf16[2,4,72,2176]{3,2,1,0:T(8,128)(2,1)}, bf16[2,4,72,2176]{3,2,1,0:T(8,128)(2,1)}, u32[]{:S(2)}, u32[]{:S(2)}) collective-permute-start(bf16[2,4,72,2176]{3,2,1,0:T(8,128)(2,1)} %bitcast.134), channel_id=1, source_target_pairs={{0,2},{1,3},{2,0},{3,1},{4,6},{5,7},{6,4},{7,5},{8,10},{9,11},{10,... | collective-permute-start | bytes 7520264 | tf_op jit(solution)/shard_map/ppermute | solution.py:68
  (216 other events, 3367.7 us)
